TPU v7x, 256 devices: a whole 4x4x8 slice. The times are simulated.
256 devices in a mesh: ctx: 128 (over z, y, x), head: 2 (over core).
Axes of the slice: x: 4, y: 4, z: 8, core: 2. Of those that a mesh axis runs over, the one named last changes fastest.
Arguments:
- queries: bfloat16 [16384, 2048], P('ctx', 'head'), may hold values from -6 to 6
- keys: bfloat16 [16384, 128], P('ctx'), may hold values from -6 to 6
- values: bfloat16 [16384, 128], P('ctx'), may hold values from -6 to 6
- d_out: bfloat16 [16384, 2048], P('ctx', 'head'), may hold values from -6 to 6
- doc_starts: int32 [16], replicated, may hold values from 0 to 15872, as said below
- assign: int32 [256], replicated, may hold values from 0 to 255, as said below
Outputs:
- attn_out: bfloat16 [16384, 2048], P('ctx', 'head')
- d_query: bfloat16 [16384, 2048], P('ctx', 'head')
- d_key: bfloat16 [16384, 128], P('ctx')
- d_value: bfloat16 [16384, 128], P('ctx')
Inputs may be any that keep to these rules, and one draw needn't show every extreme that they name: `doc_starts`: increasing multiples of 512 beginning with 0; document i runs from entry i to the next entry, the last one to 16384. A permutation: storage span c of every sequence array holds the positions assign[c] * 64 to assign[c] * 64 + 63.
All inputs are finite; a program needn't handle non-finite values.
Results may differ from a plain program's by a relative error of at most 0.035.
Values may be sent and summed in bfloat16 or wider, within the bound.
A program may use at most 128 MiB of HBM per device.

v0:
```python
import math

import jax
import jax.numpy as jnp
from jax import lax
from jax.sharding import PartitionSpec as P

HD = 128
KEY_BLOCK = 512
SPAN = 64


masked_value = -1e30


def contract_rows(left, right):
    return lax.dot_general(
        left, right, (((0,), (0,)), ((), ())), preferred_element_type=jnp.float32
    )


def contract_cols(left, right):
    return lax.dot_general(
        left, right, (((1,), (1,)), ((), ())), preferred_element_type=jnp.float32
    )


def span_pass(q_rows, g_rows, q_place, doc_first, first_block, last_block, kv_sorted, key_terms):
    score_scale = 1.0 / math.sqrt(HD)
    block_keys = jnp.arange(KEY_BLOCK, dtype=jnp.int32)
    rows_count = q_rows.shape[0]

    def score_tile(block_index):
        key_tile = lax.dynamic_slice_in_dim(kv_sorted, block_index * KEY_BLOCK, KEY_BLOCK, 0)
        scores = contract_cols(q_rows, key_tile[:, :HD]) * score_scale
        key_place = block_index * KEY_BLOCK + block_keys
        allowed = (key_place[None, :] >= doc_first) & (key_place[None, :] <= q_place[:, None])
        return (key_tile, scores, allowed)

    def stats_step(block_index, state_now):
        running_max, running_sum = state_now
        key_tile, scores, allowed = score_tile(block_index)
        scores = jnp.where(allowed, scores, masked_value)
        new_max = jnp.maximum(running_max, jnp.max(scores, axis=1))
        weights = jnp.where(allowed, jnp.exp(scores - new_max[:, None]), 0.0)
        return (new_max, running_sum * jnp.exp(running_max - new_max) + jnp.sum(weights, axis=1))

    start_state = (
        jnp.full((rows_count,), masked_value, jnp.float32),
        jnp.zeros((rows_count,), jnp.float32),
    )
    running_max, running_sum = lax.fori_loop(first_block, last_block, stats_step, start_state)
    log_total = running_max + jnp.log(running_sum)

    def probs_of(scores, allowed):
        return jnp.where(allowed, jnp.exp(scores - log_total[:, None]), 0.0).astype(jnp.bfloat16)

    def output_step(block_index, attn_acc):
        key_tile, scores, allowed = score_tile(block_index)
        return attn_acc + jnp.dot(
            probs_of(scores, allowed), key_tile[:, HD:], preferred_element_type=jnp.float32
        )

    attn_acc = lax.fori_loop(
        first_block, last_block, output_step, jnp.zeros((rows_count, HD), jnp.float32)
    )
    attn_rows = attn_acc.astype(jnp.bfloat16)
    delta_rows = jnp.sum(g_rows.astype(jnp.float32) * attn_rows.astype(jnp.float32), axis=1)

    def grad_step(block_index, state_now):
        query_acc, term_acc = state_now
        key_tile, scores, allowed = score_tile(block_index)
        probs = probs_of(scores, allowed)
        d_probs = contract_cols(g_rows, key_tile[:, HD:])
        d_scores = (
            probs.astype(jnp.float32) * (d_probs - delta_rows[:, None]) * score_scale
        ).astype(jnp.bfloat16)
        query_acc = query_acc + jnp.dot(
            d_scores, key_tile[:, :HD], preferred_element_type=jnp.float32
        )
        update = jnp.concatenate(
            [contract_rows(d_scores, q_rows), contract_rows(probs, g_rows)], axis=1
        )
        previous = lax.dynamic_slice_in_dim(term_acc, block_index * KEY_BLOCK, KEY_BLOCK, 0)
        term_acc = lax.dynamic_update_slice_in_dim(
            term_acc, previous + update, block_index * KEY_BLOCK, 0
        )
        return (query_acc, term_acc)

    start_grads = (jnp.zeros((rows_count, HD), jnp.float32), key_terms)
    query_acc, key_terms = lax.fori_loop(first_block, last_block, grad_step, start_grads)
    return (attn_rows, query_acc.astype(jnp.bfloat16), key_terms)


def body(queries, keys, values, d_out, doc_starts, assign):
    rows_dev = queries.shape[0]
    heads_dev = queries.shape[1] // HD
    spans_dev = rows_dev // SPAN
    span_total = assign.shape[0]
    tokens = span_total * SPAN
    kv_local = jnp.concatenate([keys, values], axis=1)
    kv_store = lax.all_gather(kv_local, "ctx", axis=0, tiled=True)
    span_order = (
        jnp.zeros((span_total,), jnp.int32).at[assign].set(jnp.arange(span_total, dtype=jnp.int32))
    )
    positions = jnp.arange(tokens, dtype=jnp.int32)
    to_storage = span_order[positions // SPAN] * SPAN + positions % SPAN
    to_position = assign[positions // SPAN] * SPAN + positions % SPAN
    kv_sorted = jnp.take(kv_store, to_storage, axis=0)
    my_spans = lax.dynamic_slice_in_dim(assign, lax.axis_index("ctx") * spans_dev, spans_dev, 0)
    q_rows_count = SPAN * heads_dev
    key_terms = jnp.zeros((tokens, 2 * HD), jnp.float32)
    out_pieces = []
    query_pieces = []
    for part_index in range(spans_dev):
        span_base = my_spans[part_index] * SPAN
        q_rows = queries[part_index * SPAN : (part_index + 1) * SPAN].reshape(q_rows_count, HD)
        g_rows = d_out[part_index * SPAN : (part_index + 1) * SPAN].reshape(q_rows_count, HD)
        q_place = span_base + jnp.arange(q_rows_count, dtype=jnp.int32) // heads_dev
        doc_first = jnp.max(jnp.where(doc_starts <= span_base, doc_starts, 0))
        first_block = doc_first // KEY_BLOCK
        last_block = (span_base + SPAN - 1) // KEY_BLOCK + 1
        attn_rows, query_rows, key_terms = span_pass(
            q_rows, g_rows, q_place, doc_first, first_block, last_block, kv_sorted, key_terms
        )
        out_pieces.append(attn_rows.reshape(SPAN, heads_dev * HD))
        query_pieces.append(query_rows.reshape(SPAN, heads_dev * HD))
    attn_out = jnp.concatenate(out_pieces, axis=0)
    d_query = jnp.concatenate(query_pieces, axis=0)
    stored_terms = jnp.take(key_terms, to_position, axis=0)
    reduced = lax.psum_scatter(stored_terms, "ctx", scatter_dimension=0, tiled=True)
    summed = lax.psum(reduced, "head").astype(jnp.bfloat16)
    return (attn_out, d_query, summed[:, :HD], summed[:, HD:])


def solution(mesh):
    placed = (P("ctx", "head"), P("ctx", None), P("ctx", None), P("ctx", "head"), P(), P())
    return jax.shard_map(
        body,
        mesh=mesh,
        in_specs=placed,
        out_specs=(P("ctx", "head"), P("ctx", "head"), P("ctx", None), P("ctx", None)),
        check_vma=False,
    )
```

profile of v0, /device:TPU:1, one launch (start us, length us, event | category | flops | bytes accessed | tf_op | source)
XLA Modules:
  0.0 1322.6 jit_solution(15363435403945269911)
XLA Ops:
  7.2 0.0 all-gather.2.cloned.1.call-start
  7.2 1.4 pad_maximum_fusion.2
  8.7 0.0 reduce-scatter.2.cloned.1.call-start
  8.7 0.8 dynamic_slice.27
  9.5 0.6 fusion.142
  11.4 1.3 fusion.133
  17.8 1.0 fusion.140
  18.8 0.1 reshape.212
  18.9 0.1 compare_select_fusion.2
  19.0 101.4 %gather_fusion.2 = s32[16384]{0:T(1024)S(1)} fusion(s32[256]{0:T(256)S(1)} %copy-done, s32[16384]{0:T(1024)S(1)} %broadcast_clamp_fusion.2), kind=kCustom, calls=%fused_computation.2 | custom fusion | bytes 196608 | tf_op jit(solution)/shard_map/gather | solution.py:108
  120.4 1.4 scatter_custom_fusion
  121.8 101.4 %gather_fusion = s32[16384]{0:T(1024)S(1)} fusion(s32[256]{0:T(256)S(1)} %scatter_custom_fusion, s32[16384]{0:T(1024)S(1)} %broadcast_clamp_fusion.2), kind=kCustom, calls=%fused_computation | custom fusion | bytes 196608 | tf_op jit(solution)/shard_map/gather | solution.py:107
  223.2 0.1 reshape.208
  223.3 0.1 reshape.210
  223.4 0.1 reshape.206
  223.6 0.1 compare_select_fusion.1
  223.7 0.1 compare_select_fusion
  223.8 0.0 all-gather.2.cloned.1.call-done
  223.9 65.3 %gather_fusion.1 = bf16[16384,256]{1,0:T(8,128)(2,1)} fusion(bf16[16384,256]{1,0:T(8,128)(2,1)} %all-gather.2.cloned.1.call-done, s32[16384]{0:T(1024)S(1)} %broadcast_clamp_fusion.1), kind=kCustom, calls=%fused_computation.1 | custom fusion | bytes 16842752 | tf_op jit(solution)/shard_map/jit(_take)/gather | solution.py:109
  289.1 8.0 broadcast_select_fusion.1
  297.2 2.4 while.76
  297.2 0.6 broadcast_compare_fusion.14
  297.8 1.3 fusion.223
  299.1 0.4 select_reduce_fusion.5
  299.6 2.2 while.77
  299.6 0.6 broadcast_compare_fusion.15
  300.2 1.6 fusion.228
  301.8 2.4 while.74
  301.9 0.7 broadcast_compare_fusion.12
  302.5 1.3 fusion.215
  303.9 0.4 select_reduce_fusion.4
  304.3 2.3 while.75
  304.3 0.7 broadcast_compare_fusion.13
  305.0 1.6 fusion.220
  306.6 0.1 multiply_reduce_fusion.1
  306.7 7.7 broadcast_in_dim.88
  314.4 7.2 while.78
  314.4 0.7 broadcast_compare_fusion.16
  315.1 1.4 fusion.240
  316.5 1.2 fusion.241
  317.7 1.3 convolution_add_fusion.4
  319.0 0.3 fusion.242
  319.3 0.3 fusion.243
  319.6 1.9 fusion.244
  321.6 0.1 multiply_reduce_fusion
  321.7 7.2 while.79
  321.8 0.6 broadcast_compare_fusion.17
  322.4 1.4 fusion.256
  323.8 1.2 fusion.257
  325.0 1.3 convolution_add_fusion.5
  326.3 0.3 fusion.258
  326.6 0.3 fusion.259
  327.0 1.9 fusion.260
  328.9 17.5 %copy.15 = f32[16384,256]{1,0:T(8,128)} copy(f32[16384,256]{0,1:T(8,128)} %get-tuple-element.335) | data formatting | bytes 33554432 | tf_op jit(solution)/shard_map/while | solution.py:91
  346.4 67.5 %gather_fusion.3 = f32[16384,256]{1,0:T(8,128)} fusion(f32[16384,256]{1,0:T(8,128)} %copy.15, s32[16384]{0:T(1024)S(1)} %broadcast_clamp_fusion), kind=kCustom, calls=%fused_computation.3 | custom fusion | bytes 33619968 | tf_op jit(solution)/shard_map/jit(_take)/gather | solution.py:130
  413.9 12.2 broadcast_select_fusion
  426.1 0.1 reshape.209
  426.1 0.1 reshape.207
  426.2 0.1 reshape.213
  426.3 0.1 reshape.211
  426.4 0.8 pad_maximum_fusion
  427.2 785.7 %reduce-scatter.2.cloned.1.call-done = f32[128,256]{1,0:T(8,128)} async-done(((f32[16384,256]{1,0:T(8,128)}), f32[128,256]{1,0:T(8,128)}) %reduce-scatter.2.cloned.1.call-update) | async-done | bytes 131088 | tf_op jit(solution)/shard_map/reduce_scatter | solution.py:131
  1212.9 102.2 %all-reduce.1 = bf16[128,256]{1,0:T(8,128)(2,1)S(1)} all-reduce(f32[128,256]{1,0:T(8,128)} %reduce-scatter.2.cloned.1.call-done), channel_id=1, replica_groups=mesh['ctx'=128,'head'=2] {'head'}, use_global_device_ids=true, to_apply=%region_22.23 | all-reduce | flops 32768 | bytes 196608 | tf_op jit(solution)/shard_map/psum | solution.py:132
  1315.1 0.6 fusion.141
  (40 shorter events, 0.4 us)
Async XLA Ops:
  7.2 11.8 copy-start
  7.2 216.7 %all-gather.2.cloned.1.call-start = ((), (), s32[]{:S(2)}) async-start(), calls=%async_computation.1 | async-start | bytes 8454144 | tf_op jit(solution)/shard_map/all_gather | solution.py:102
  8.7 1204.3 %reduce-scatter.2.cloned.1.call-start = ((), (), s32[]{:S(2)}) async-start(), calls=%async_computation.2 | async-start | bytes 16908288 | tf_op jit(solution)/shard_map/reduce_scatter | solution.py:131
  121.8 101.4 %copy-start.1 = (bf16[128,1024]{1,0:T(8,128)(2,1)S(1)}, bf16[128,1024]{1,0:T(8,128)(2,1)}, u32[]{:S(2)}) copy-start(bf16[128,1024]{1,0:T(8,128)(2,1)} %param.18) | copy-start | bytes 786436
Sparse Core Ops, SparseCore 0:
  12.2 124.9 all-gather.1
  426.2 786.6 reduce-scatter.1
where the time goes:
time: 1330 us; the launch traced here: 1320 us
  waiting for transfers between devices  786 us (59%)
  local copies, waits for them, and re-layouts  366 us (28%)
  blocking collectives  102 us (8%)
  other arithmetic  33 us (2%)
  between operations  20.9 us (2%)
  matrix products  14.8 us (1%)
    reduce_scatter x1, waiting for transfers between devices, body(): lax.psum_scatter(stored_terms, 'ctx', scatter_dimension=0, tiled=True)  786 us
    psum x1, blocking collectives, body(): summed = lax.psum(reduced, 'head').astype(jnp.bfloat16)  102 us
    gather x1, local copies, waits for them, and re-layouts, body(): to_position = assign[positions // SPAN] * SPAN + positions % SPAN  101 us
    gather x1, local copies, waits for them, and re-layouts, body(): to_storage = span_order[positions // SPAN] * SPAN + positions % SPAN  101 us
    gather x1, local copies, waits for them, and re-layouts, body(): stored_terms = jnp.take(key_terms, to_position, axis=0)  67.5 us
    gather x1, local copies, waits for them, and re-layouts, body(): kv_sorted = jnp.take(kv_store, to_storage, axis=0)  65.3 us
  transfers between devices with their start and end apart: 2, of which 1 were waited for; matrix products, arithmetic and copies ran while one was open for 16% of the time, Pallas kernels for 0%

commit v1 on v0

v1 whole, which is shorter than its diff:
```python
import functools
import math

import jax
import jax.numpy as jnp
from jax import lax
from jax.experimental import pallas as pl
from jax.experimental.pallas import tpu as pltpu
from jax.sharding import PartitionSpec as P

HD = 128
SPAN = 64
BLOCK = 512
UNIT = 512
MESH = pl.DeviceIdType.MESH
AXES = ("z", "y", "x")
SIZES = {"z": 8, "y": 4, "x": 4}
PARTS = (
    (0, 32, ("y", "x", "z")),
    (32, 48, ("z", "y", "x")),
    (80, 48, ("z", "x", "y")),
)
VMEM_BYTES = 60 * 1024 * 1024


def my_place():
    me = lax.axis_index("ctx")
    nx, ny = SIZES["x"], SIZES["y"]
    pos = {"x": lax.rem(me, nx), "y": lax.rem(me // nx, ny), "z": me // (nx * ny)}
    return pos, me, lax.axis_index("head")


def wrapped(value, size):
    return lax.rem(value + 2 * size, size)


def ring_peer(pos, core, axis, step):
    there = dict(pos)
    there[axis] = wrapped(pos[axis] + step, SIZES[axis])
    return ((there["z"] * SIZES["y"] + there["y"]) * SIZES["x"] + there["x"], core)


def greet(pos, me, core):
    barrier = pltpu.get_barrier_semaphore()
    for axis in AXES:
        for step in (1, -1):
            pl.semaphore_signal(
                barrier, inc=1, device_id=ring_peer(pos, core, axis, step), device_id_type=MESH
            )
    pl.semaphore_signal(barrier, inc=1, device_id=(me, 1 - core), device_id_type=MESH)
    pl.semaphore_wait(barrier, 2 * len(AXES) + 1)


def row_half(first, count, side):
    low = count // 32 * 16 if count % 32 == 0 else (count // 32 + 1) * 16
    return (first, low) if side == 0 else (first + low, count - low)


def axis_half(axis, side):
    half = SIZES[axis] // 2
    return (side * half, half)


def spans(sel):
    return tuple(pl.ds(first, count) for first, count in sel)


def gather_view(pos, part, stage, index, half):
    first, count, order = PARTS[part]
    sel = {}
    for rank, axis in enumerate(order):
        if rank < stage:
            sel[axis] = (0, SIZES[axis])
        elif rank == stage:
            sel[axis] = (index, 1)
        else:
            sel[axis] = (pos[axis], 1)
    rows = (first, count)
    if half is not None:
        if stage == 0:
            rows = row_half(first, count, half)
        else:
            sel[order[0]] = axis_half(order[0], half)
    return spans([sel[axis] for axis in AXES] + [rows])


def ring_steps(order):
    return [(stage, step) for stage, axis in enumerate(order) for step in range(1, SIZES[axis] // 2 + 1)]


def gather_kernel(kv_ref, all_ref, send, recv, side_send, side_recv, local_sem):
    pos, me, core = my_place()
    greet(pos, me, core)
    mine = pltpu.make_async_copy(
        kv_ref, all_ref.at[:, pl.ds(pos["z"], 1), pl.ds(pos["y"], 1), pl.ds(pos["x"], 1)], local_sem
    )
    mine.start()

    def copy(part, stage, step, way, arriving):
        order = PARTS[part][2]
        axis = order[stage]
        toward = 1 - 2 * way
        index = wrapped(pos[axis] - toward * (step if arriving else step - 1), SIZES[axis])
        half = way if step == SIZES[axis] // 2 else None
        view = gather_view(pos, part, stage, index, half)
        src = all_ref.at[(core, *view)]
        if not arriving and stage == 0 and step == 1:
            src = kv_ref.at[(core, pl.ds(0, 1), pl.ds(0, 1), pl.ds(0, 1), view[3])]
        return pltpu.make_async_remote_copy(
            src_ref=src,
            dst_ref=all_ref.at[(core, *view)],
            send_sem=send.at[part, stage, step - 1, way],
            recv_sem=recv.at[part, stage, step - 1, way],
            device_id=ring_peer(pos, core, axis, toward),
            device_id_type=MESH,
        )

    def side_copy(part, stage, step, way, owner):
        axis = PARTS[part][2][stage]
        toward = 1 - 2 * way
        index = wrapped(pos[axis] - toward * step, SIZES[axis])
        half = way if step == SIZES[axis] // 2 else None
        view = gather_view(pos, part, stage, index, half)
        return pltpu.make_async_remote_copy(
            src_ref=all_ref.at[(owner, *view)],
            dst_ref=all_ref.at[(owner, *view)],
            send_sem=side_send.at[part, stage, step - 1, way],
            recv_sem=side_recv.at[part, stage, step - 1, way],
            device_id=(me, 1 - core),
            device_id_type=MESH,
        )

    plans = [ring_steps(order) for _, _, order in PARTS]
    longest = max(len(plan) for plan in plans)
    for slot in range(longest + 1):
        for part, plan in enumerate(plans):
            if slot > len(plan):
                continue
            if slot > 0:
                for way in (0, 1):
                    copy(part, *plan[slot - 1], way, True).wait_recv()
            if slot < len(plan):
                for way in (0, 1):
                    copy(part, *plan[slot], way, False).start()
            if slot > 0:
                for way in (0, 1):
                    side_copy(part, *plan[slot - 1], way, core).start()
        if slot == 0:
            mine.wait()
    for part, plan in enumerate(plans):
        for stage, step in plan:
            for way in (0, 1):
                copy(part, stage, step, way, False).wait_send()
                side_copy(part, stage, step, way, core).wait_send()
                side_copy(part, stage, step, way, 1 - core).wait_recv()


def gather_all(kv):
    dims = tuple(SIZES[axis] for axis in AXES)
    sems = pltpu.SemaphoreType.DMA((len(PARTS), 3, 4, 2))
    return pl.pallas_call(
        gather_kernel,
        out_shape=jax.ShapeDtypeStruct((2, *dims, 2 * SPAN, HD), jnp.bfloat16),
        in_specs=[pl.BlockSpec(memory_space=pl.ANY)],
        out_specs=pl.BlockSpec(memory_space=pl.ANY),
        scratch_shapes=[sems, sems, sems, sems, pltpu.SemaphoreType.DMA],
        compiler_params=pltpu.CompilerParams(collective_id=0, has_side_effects=True),
    )(kv)


def sum_views(pos, part, stage, index, half):
    first, count, gather_order = PARTS[part]
    order = gather_order[::-1]
    held, landed = {}, {}
    for rank, axis in enumerate(order):
        if rank < stage:
            held[axis], landed[axis] = (pos[axis], 1), (0, 1)
        elif rank == stage:
            held[axis] = landed[axis] = (index, 1)
        else:
            held[axis] = landed[axis] = (0, SIZES[axis])
    rows = (0, count)
    if half is not None:
        if stage == 2:
            rows = row_half(0, count, half)
        else:
            held[order[2]] = landed[order[2]] = axis_half(order[2], half)
    return (
        [held[axis] for axis in AXES] + [(first + rows[0], rows[1])],
        [landed[axis] for axis in AXES] + [rows],
    )


def landing_shape(part, stage):
    _, count, gather_order = PARTS[part]
    order = gather_order[::-1]
    dims = tuple(1 if order.index(axis) < stage else SIZES[axis] for axis in AXES)
    return (2, *dims, count, HD)


def each_chunk(counts, body):
    widest = max(range(3), key=lambda i: counts[i])
    others = [i for i in range(3) if i != widest]

    def step(at, carry):
        for a in range(counts[others[0]]):
            for b in range(counts[others[1]]):
                place = [None] * 3
                place[widest], place[others[0]], place[others[1]] = at, a, b
                body(place)
        return carry

    if counts[widest] == 1:
        step(0, 0)
    else:
        lax.fori_loop(0, counts[widest], step, 0)


def chunk_of(sel, place, lead=()):
    return (*lead, *(first + at for (first, _), at in zip(sel, place)), pl.ds(*sel[3]), slice(None))


def as_f32(value):
    return value.astype(jnp.float32)


def reduce_kernel(*refs):
    terms_ref, out_ref, held, other, final = refs[:5]
    landing = {}
    at = 5
    for part in range(len(PARTS)):
        for stage in range(3):
            landing[part, stage] = refs[at]
            at += 1
    send, recv, load_sem, side_send, side_recv, last_send, last_recv = refs[at:]
    pos, me, core = my_place()
    sibling = (me, 1 - core)
    greet(pos, me, core)

    def load(z):
        return pltpu.make_async_copy(terms_ref.at[core, z], held.at[z], load_sem.at[z])

    def side(z):
        return pltpu.make_async_remote_copy(
            src_ref=terms_ref.at[1 - core, z],
            dst_ref=other.at[z],
            send_sem=side_send.at[z],
            recv_sem=side_recv.at[z],
            device_id=sibling,
            device_id_type=MESH,
        )

    for z in range(SIZES["z"]):
        side(z).start()
        load(z).start()
    for z in range(SIZES["z"]):
        load(z).wait()
        side(z).wait_recv()

        def join(place, z=z):
            where = (z, place[1], place[2])
            held[where] = (as_f32(held[where]) + as_f32(other[where])).astype(jnp.bfloat16)

        each_chunk((1, SIZES["y"], SIZES["x"]), join)

    def copy(part, stage, step, way, arriving):
        axis = PARTS[part][2][::-1][stage]
        toward = 1 - 2 * way
        size = SIZES[axis]
        reach = size // 2 - step + (0 if arriving else 1)
        index = wrapped(pos[axis] + toward * reach, size)
        half = way if step == 1 else None
        from_sel, to_sel = sum_views(pos, part, stage, index, half)
        return pltpu.make_async_remote_copy(
            src_ref=held.at[spans(from_sel)],
            dst_ref=landing[part, stage].at[(way, *spans(to_sel))],
            send_sem=send.at[part, stage, step - 1, way],
            recv_sem=recv.at[part, stage, step - 1, way],
            device_id=ring_peer(pos, core, axis, toward),
            device_id_type=MESH,
        )

    def add_arrived(part, stage, step, way):
        axis = PARTS[part][2][::-1][stage]
        toward = 1 - 2 * way
        size = SIZES[axis]
        index = wrapped(pos[axis] + toward * (size // 2 - step), size)
        half = way if step == 1 else None
        into, arrived = sum_views(pos, part, stage, index, half)
        landed = landing[part, stage]

        def add(place):
            where = chunk_of(into, place)
            more = landed[chunk_of(arrived, place, (way,))]
            held[where] = (as_f32(held[where]) + as_f32(more)).astype(jnp.bfloat16)

        each_chunk([count for _, count in into[:3]], add)

    def add_both(part, stage, step):
        axis = PARTS[part][2][::-1][stage]
        into, arrived = sum_views(pos, part, stage, pos[axis], None)
        landed = landing[part, stage]

        def add(place):
            where = chunk_of(into, place)
            total = as_f32(held[where])
            total = total + as_f32(landed[chunk_of(arrived, place, (0,))])
            total = total + as_f32(landed[chunk_of(arrived, place, (1,))])
            held[where] = total.astype(jnp.bfloat16)

        each_chunk([count for _, count in into[:3]], add)

    plans = [ring_steps(order[::-1]) for _, _, order in PARTS]
    longest = max(len(plan) for plan in plans)
    for slot in range(longest + 1):
        for part, plan in enumerate(plans):
            if slot > len(plan):
                continue
            if slot > 0:
                stage, step = plan[slot - 1]
                for way in (0, 1):
                    copy(part, stage, step, way, True).wait_recv()
                last_step = step == SIZES[PARTS[part][2][::-1][stage]] // 2
                if last_step and step > 1:
                    add_both(part, stage, step)
                else:
                    for way in (0, 1):
                        add_arrived(part, stage, step, way)
            if slot < len(plan):
                for way in (0, 1):
                    copy(part, *plan[slot], way, False).start()

    final[core] = held[pos["z"], pos["y"], pos["x"]]
    last = pltpu.make_async_remote_copy(
        src_ref=final.at[core],
        dst_ref=final.at[core],
        send_sem=last_send,
        recv_sem=last_recv,
        device_id=sibling,
        device_id_type=MESH,
    )
    last.start()
    for z in range(SIZES["z"]):
        side(z).wait_send()
    for part, plan in enumerate(plans):
        for stage, step in plan:
            for way in (0, 1):
                copy(part, stage, step, way, False).wait_send()
    last.wait()
    out_ref[...] = final[...]


def reduce_all(terms):
    dims = tuple(SIZES[axis] for axis in AXES)
    whole = pltpu.VMEM((*dims, 2 * SPAN, HD), jnp.bfloat16)
    sems = pltpu.SemaphoreType.DMA((len(PARTS), 3, 4, 2))
    by_z = pltpu.SemaphoreType.DMA((SIZES["z"],))
    return pl.pallas_call(
        reduce_kernel,
        out_shape=jax.ShapeDtypeStruct((2, 2 * SPAN, HD), jnp.bfloat16),
        in_specs=[pl.BlockSpec(memory_space=pl.ANY)],
        out_specs=pl.BlockSpec(memory_space=pltpu.VMEM),
        scratch_shapes=[whole, whole, pltpu.VMEM((2, 2 * SPAN, HD), jnp.bfloat16)]
        + [
            pltpu.VMEM(landing_shape(part, stage), jnp.bfloat16)
            for part in range(len(PARTS))
            for stage in range(3)
        ]
        + [sems, sems, by_z, by_z, by_z, pltpu.SemaphoreType.DMA, pltpu.SemaphoreType.DMA],
        compiler_params=pltpu.CompilerParams(
            collective_id=1, has_side_effects=True, vmem_limit_bytes=VMEM_BYTES
        ),
    )(terms)


def dot(left, right, contract):
    return lax.dot_general(
        left, right, ((contract[:1], contract[1:]), ((), ())), preferred_element_type=jnp.float32
    )


def attention_kernel(
    place_ref, starts_ref, spans_ref, q_ref, g_ref, kv_ref, out_ref, dq_ref, terms_ref,
    scores, probs, q_cols, g_cols, acc,
):
    heads = q_ref.shape[1] // HD
    cols = heads * SPAN
    scale = 1.0 / math.sqrt(HD)
    to_exp2 = scale * math.log2(math.e)
    per_block = BLOCK // SPAN

    def clear(at, carry):
        terms_ref[:, pl.ds(pl.multiple_of(at * 256, 256), 256), :] = jnp.zeros((2, 256, HD), jnp.bfloat16)
        return carry

    lax.fori_loop(0, terms_ref.shape[1] // 256, clear, 0)

    for part in range(2):
        base = spans_ref[part] * SPAN
        doc_first = jnp.int32(0)
        for doc in range(starts_ref.shape[0]):
            start = starts_ref[doc]
            doc_first = jnp.where(start <= base, jnp.maximum(doc_first, start), doc_first)
        first_block = doc_first // BLOCK
        full_blocks = base // BLOCK - first_block
        inside = base - (base // BLOCK) * BLOCK

        rows = pl.ds(part * SPAN, SPAN)
        q_rows = jnp.concatenate(
            [q_ref[rows, h * HD : (h + 1) * HD] for h in range(heads)], axis=0
        )
        g_rows = jnp.concatenate(
            [g_ref[rows, h * HD : (h + 1) * HD] for h in range(heads)], axis=0
        )
        q_t = as_f32(q_rows).T
        g_t = as_f32(g_rows).T
        q_cols[...] = q_t.astype(jnp.bfloat16)
        g_cols[...] = g_t.astype(jnp.bfloat16)

        def row_of(block, i):
            span = place_ref[(first_block + block) * per_block + i]
            return pl.ds(pl.multiple_of(span * SPAN, SPAN), SPAN)

        def tile(which, block):
            return jnp.concatenate(
                [kv_ref[which, row_of(block, i), :] for i in range(per_block)], axis=0
            )

        def fold(value, op):
            value = value.reshape(BLOCK // 8, 8, cols)
            return op(value, axis=0)

        def score_step(block, top):
            s = dot(tile(0, block), q_cols[...], (1, 0))
            scores[block] = s
            return jnp.maximum(top, fold(s, jnp.max))

        top = lax.fori_loop(0, full_blocks, score_step, jnp.full((8, cols), -1e30, jnp.float32))
        s = dot(tile(0, full_blocks), q_cols[...], (1, 0))
        key_at = lax.broadcasted_iota(jnp.int32, (BLOCK, cols), 0)
        query_at = lax.broadcasted_iota(jnp.int32, (BLOCK, cols), 1)
        s = jnp.where(key_at <= inside + lax.rem(query_at, SPAN), s, -1e30)
        scores[full_blocks] = s
        top = jnp.max(jnp.maximum(top, fold(s, jnp.max)), axis=0, keepdims=True)

        acc[...] = jnp.zeros_like(acc)

        def value_step(block, total):
            p = jnp.exp2((scores[block] - top) * to_exp2)
            p16 = p.astype(jnp.bfloat16)
            probs[block] = p16
            acc[...] += dot(tile(1, block), p16, (0, 0))
            return total + fold(p, jnp.sum)

        total = lax.fori_loop(0, full_blocks + 1, value_step, jnp.zeros((8, cols), jnp.float32))
        inverse = 1.0 / jnp.sum(total, axis=0, keepdims=True)
        out_t = (acc[...] * inverse).astype(jnp.bfloat16).astype(jnp.float32)
        delta = jnp.sum(g_t * out_t, axis=0, keepdims=True)
        q_scaled = (q_t * (inverse * scale)).astype(jnp.bfloat16)
        g_scaled = (g_t * inverse).astype(jnp.bfloat16)
        out_rows = out_t.T.astype(jnp.bfloat16)
        acc[...] = jnp.zeros_like(acc)

        def grad_step(block, carry):
            p16 = probs[block]
            keys = tile(0, block)
            d_probs = dot(tile(1, block), g_cols[...], (1, 0))
            d_scores = (as_f32(p16) * (d_probs - delta)).astype(jnp.bfloat16)
            acc[...] += dot(keys, d_scores, (0, 0))
            d_key = dot(d_scores, q_scaled, (1, 1))
            d_value = dot(p16, g_scaled, (1, 1))
            for i in range(per_block):
                at = row_of(block, i)
                for which, term in ((0, d_key), (1, d_value)):
                    piece = term[i * SPAN : (i + 1) * SPAN]
                    if part > 0:
                        piece = piece + as_f32(terms_ref[which, at, :])
                    terms_ref[which, at, :] = piece.astype(jnp.bfloat16)
            return carry

        lax.fori_loop(0, full_blocks + 1, grad_step, 0)
        dq_rows = (acc[...] * (inverse * scale)).T.astype(jnp.bfloat16)
        for h in range(heads):
            out_ref[rows, h * HD : (h + 1) * HD] = out_rows[h * SPAN : (h + 1) * SPAN]
            dq_ref[rows, h * HD : (h + 1) * HD] = dq_rows[h * SPAN : (h + 1) * SPAN]


def attention(place, doc_starts, my_spans, queries, d_out, kv_all):
    tokens = kv_all.shape[1]
    heads = queries.shape[1] // HD
    cols = heads * SPAN
    longest = tokens - (doc_starts.shape[0] - 1) * UNIT
    blocks = -(-longest // BLOCK)
    smem = pl.BlockSpec(memory_space=pltpu.SMEM)
    vmem = pl.BlockSpec(memory_space=pltpu.VMEM)
    return pl.pallas_call(
        attention_kernel,
        out_shape=(
            jax.ShapeDtypeStruct(queries.shape, jnp.bfloat16),
            jax.ShapeDtypeStruct(queries.shape, jnp.bfloat16),
            jax.ShapeDtypeStruct((2, tokens, HD), jnp.bfloat16),
        ),
        in_specs=[smem, smem, smem, vmem, vmem, vmem],
        out_specs=(vmem, vmem, vmem),
        scratch_shapes=[
            pltpu.VMEM((blocks, BLOCK, cols), jnp.float32),
            pltpu.VMEM((blocks, BLOCK, cols), jnp.bfloat16),
            pltpu.VMEM((HD, cols), jnp.bfloat16),
            pltpu.VMEM((HD, cols), jnp.bfloat16),
            pltpu.VMEM((HD, cols), jnp.float32),
        ],
        compiler_params=pltpu.CompilerParams(vmem_limit_bytes=VMEM_BYTES),
    )(place, doc_starts, my_spans, queries, d_out, kv_all)


def body(queries, keys, values, d_out, doc_starts, assign):
    span_total = assign.shape[0]
    tokens = span_total * SPAN
    rows_dev = queries.shape[0]
    dims = tuple(SIZES[axis] for axis in AXES)
    kv = jnp.stack([keys, values]).reshape(2, 1, 1, 1, rows_dev, HD)
    ids = jnp.arange(span_total, dtype=jnp.int32)
    place = jnp.sum(jnp.where(assign[None, :] == ids[:, None], ids[None, :], 0), axis=1)
    my_spans = lax.dynamic_slice_in_dim(assign, lax.axis_index("ctx") * 2, 2, 0)
    kv_all = gather_all(kv).reshape(2, tokens, HD)
    attn_out, d_query, terms = attention(place, doc_starts, my_spans, queries, d_out, kv_all)
    summed = reduce_all(terms.reshape(2, *dims, rows_dev, HD))
    return (attn_out, d_query, summed[0], summed[1])


def solution(mesh):
    placed = (P("ctx", "head"), P("ctx", None), P("ctx", None), P("ctx", "head"), P(), P())
    return jax.shard_map(
        body,
        mesh=mesh,
        in_specs=placed,
        out_specs=(P("ctx", "head"), P("ctx", "head"), P("ctx", None), P("ctx", None)),
        check_vma=False,
    )
```

time: 1330 us -> 129 us (0.10)
  waiting for transfers between devices: 786 us -> 0 us
  local copies, waits for them, and re-layouts: 366 us -> 2.67 us
  Pallas kernels: 0 us -> 123 us
  blocking collectives: 102 us -> 0 us
  other arithmetic: 33 us -> 2.77 us
  between operations: 20.9 us -> 0.65 us
  matrix products: 14.8 us -> 0 us
    reduce_scatter x1 -> x0, waiting for transfers between devices: 786 us -> none  [body(): lax.psum_scatter(stored_terms, 'ctx', scatter_dimension=0, tiled=True)]
    gather x4 -> x0, local copies, waits for them, and re-layouts: 336 us -> none  [the longest x1 101 us: body(): to_position = assign[positions // SPAN] * SPAN + positions % SPAN]
    pallas_call x0 -> x3, Pallas kernels: none -> 123 us  [the longest x1 55.5 us: gather_all(): pl.pallas_call(gather_kernel, out_shape=jax.ShapeDtypeStruct((2, *dims, 2...]
    psum x1 -> x0, blocking collectives: 102 us -> none  [body(): summed = lax.psum(reduced, 'head').astype(jnp.bfloat16)]
    select_n x6 -> x0, other arithmetic: 20.5 us -> none  [the longest x2 12.3 us: body(): stored_terms = jnp.take(key_terms, to_position, axis=0)]
    while x3 -> x0, local copies, waits for them, and re-layouts: 17.5 us -> none  [the longest x1 17.5 us: span_pass(): lax.fori_loop(first_block, last_block, grad_step, start_grads)]
    dot_general x14 -> x0, matrix products: 14.8 us -> none  [the longest x6 7.85 us: contract_cols(): lax.dot_general(left, right, (((1,), (1,)), ((), ())), preferred_element_...]
  transfers between devices with their start and end apart: 2 -> 0, of which waited for: 1 -> 0; matrix products, arithmetic and copies ran while one was open for 16% -> 0% of each run, Pallas kernels for 0% -> 0%
where the time goes in v1:
time: 129 us
  Pallas kernels  123 us (95%)
  other arithmetic  2.77 us (2%)
  local copies, waits for them, and re-layouts  2.67 us (2%)
    pallas_call x1, Pallas kernels, gather_all(): pl.pallas_call(gather_kernel, out_shape=jax.ShapeDtypeStruct((2, *dims, 2...  55.5 us
    pallas_call x1, Pallas kernels, reduce_all(): pl.pallas_call(reduce_kernel, out_shape=jax.ShapeDtypeStruct((2, 2 * SPAN...  54.3 us
    pallas_call x1, Pallas kernels, attention(): pl.pallas_call(attention_kernel, out_shape=(jax.ShapeDtypeStruct(queries....  13.1 us

profile of v1, /device:TPU:1, one launch (start us, length us, event | category | flops | bytes accessed | tf_op | source)
XLA Modules:
  0.0 129.0 jit_solution(2899565426265433288)
XLA Ops:
  0.6 1.3 dynamic_slice.3.spans_ref
  1.9 1.4 %select_reduce_fusion.place_ref = s32[256]{0:T(256)} fusion(s32[256]{0:T(256)} %param.11), kind=kLoop, calls=%fused_computation | loop fusion | flops 196352 | bytes 2048 | tf_op jit(solution)/shard_map/reduce_sum | solution.py:523
  3.3 1.4 %maximum_bitcast_fusion.kv_ref = bf16[2,1,1,1,128,128]{5,4,3,2,1,0:T(8,128)(2,1)} fusion(bf16[1,128,128]{2,1,0:T(8,128)(2,1)} %bitcast.12, bf16[1,128,128]{2,1,0:T(8,128)(2,1)} %bitcast.13), kind=kLoop, calls=%fused_computation.2 | loop fusion | flops 32768 | bytes 131072 | tf_op jit(solution)/shard_map/reshape | solution.py:521
  4.7 55.5 %shard_map.93 = bf16[2,8,4,4,128,128]{5,4,3,2,1,0:T(8,128)(2,1)} custom-call(bf16[2,1,1,1,128,128]{5,4,3,2,1,0:T(8,128)(2,1)} %maximum_bitcast_fusion.kv_ref), custom_call_target="tpu_custom_call" | custom-call | tf_op jit(solution)/shard_map/pallas_call | solution.py:161
  60.2 13.1 %shard_map.94 = (bf16[128,1024]{1,0:T(8,128)(2,1)}, bf16[128,1024]{1,0:T(8,128)(2,1)}, bf16[2,16384,128]{2,1,0:T(8,128)(2,1)}) custom-call(s32[256]{0:T(256)} %select_reduce_fusion.place_ref, s32[16]{0:T(128)} %starts_ref.1, s32[2]{0:T(128)} %dynamic_slice.3.spans_ref, bf16[128,1024]{1,0:T(8,128)(2,1)} %q_ref.1, bf16[128,1024]{1,0:T(8,128)(2,1)} %g_ref.1, ...), custom_call_target="tpu_custom_call" | custom-call | tf_op jit(solution)/shard_map/pallas_call | solution.py:496
  73.3 54.3 %shard_map.95 = bf16[2,128,128]{2,1,0:T(8,128)(2,1)} custom-call(bf16[2,8,4,4,128,128]{5,4,3,2,1,0:T(8,128)(2,1)} %bitcast.11), custom_call_target="tpu_custom_call" | custom-call | tf_op jit(solution)/shard_map/pallas_call | solution.py:358
  127.6 1.4 %slice_bitcast_fusion = (bf16[128,128]{1,0:T(8,128)(2,1)}, bf16[128,128]{1,0:T(8,128)(2,1)}) fusion(bf16[2,128,128]{2,1,0:T(8,128)(2,1)} %shard_map.95), kind=kLoop, calls=%fused_computation.3 | loop fusion | bytes 131072 | tf_op jit(solution)/shard_map/squeeze | solution.py:528

commit v2 on v0

v2 whole, which is shorter than its diff:
```python
import math

import jax
import jax.numpy as jnp
from jax import lax
from jax.experimental import pallas as pl
from jax.experimental.pallas import tpu as pltpu
from jax.sharding import PartitionSpec as P

HD = 128
SPAN = 64
ROWS = 2 * SPAN
BLOCK = 512
UNIT = 512
MESH = pl.DeviceIdType.MESH
AXES = ("z", "y", "x")
SIZES = {"z": 8, "y": 4, "x": 4}
ROUTE_A = (0, 32)
ROUTES = ((32, 48, "y", "x"), (80, 48, "x", "y"))
NEAR = (1, -1, 2)
Z_AWAY = (1, -1, 2, -2, 3, -3, 4)
GROUPS = ((0,), (1, -1), (2, -2), (3, -3), (4,))
COPIES = 160
VMEM_BYTES = 60 * 1024 * 1024


def my_place():
    me = lax.axis_index("ctx")
    nx, ny = SIZES["x"], SIZES["y"]
    pos = {"x": lax.rem(me, nx), "y": lax.rem(me // nx, ny), "z": me // (nx * ny)}
    return pos, me, lax.axis_index("head")


def wrapped(value, size):
    return lax.rem(value + 2 * size, size)


def shifted(pos, axis, step):
    return wrapped(pos[axis] + step, SIZES[axis])


def peer(pos, core, axis, step):
    there = dict(pos)
    there[axis] = shifted(pos, axis, step)
    return ((there["z"] * SIZES["y"] + there["y"]) * SIZES["x"] + there["x"], core)


def greet(pos, me, core):
    barrier = pltpu.get_barrier_semaphore()
    partners = [("z", step) for step in Z_AWAY] + [(axis, step) for axis in "yx" for step in NEAR]
    for axis, step in partners:
        pl.semaphore_signal(
            barrier, inc=1, device_id=peer(pos, core, axis, step), device_id_type=MESH
        )
    pl.semaphore_signal(barrier, inc=1, device_id=(me, 1 - core), device_id_type=MESH)
    pl.semaphore_wait(barrier, len(partners) + 1)


def as_f32(value):
    return value.astype(jnp.float32)


class Numbers(dict):
    def __missing__(self, key):
        self[key] = len(self)
        assert len(self) <= COPIES
        return self[key]


def gather_kernel(k_ref, v_ref, all_ref, send, recv, side_send, side_recv, local_sem):
    pos, me, core = my_place()
    here = tuple(pl.ds(pos[axis], 1) for axis in AXES)
    own_copies = [
        pltpu.make_async_copy(ref, all_ref.at[(which, *here)], local_sem.at[which])
        for which, ref in ((0, k_ref), (1, v_ref))
    ]
    for copy in own_copies:
        copy.start()
    greet(pos, me, core)
    for copy in own_copies:
        copy.wait()

    number = Numbers()
    started, passed = [], []

    def view(owner, rows, **sel):
        index = [sel[axis] if axis in sel else (pos[axis], 1) for axis in AXES]
        return all_ref.at[(owner, *(pl.ds(*at) for at in index), pl.ds(*rows), slice(None))]

    def copy(key, axis, step, rows, sel):
        ref = view(core, rows, **sel)
        at = number[key]
        return pltpu.make_async_remote_copy(
            src_ref=ref, dst_ref=ref, send_sem=send.at[at], recv_sem=recv.at[at],
            device_id=peer(pos, core, axis, step), device_id_type=MESH,
        )

    def side(key, owner, rows, sel):
        ref = view(owner, rows, **sel)
        at = number[key]
        return pltpu.make_async_remote_copy(
            src_ref=ref, dst_ref=ref, send_sem=side_send.at[at], recv_sem=side_recv.at[at],
            device_id=(me, 1 - core), device_id_type=MESH,
        )

    def push(key, axis, step, rows, sel):
        copy(key, axis, step, rows, sel).start()
        started.append((key, axis, step, rows, sel))

    def arrive(key, axis, step, rows, sel):
        copy(key, axis, step, rows, sel).wait_recv()
        side(key, core, rows, sel).start()
        passed.append((key, rows, sel))

    def full(axis):
        return (0, SIZES[axis])

    def half(axis, side_at):
        return (side_at * (SIZES[axis] // 2), SIZES[axis] // 2)

    def from_z(route, d):
        first, count, _, _ = ROUTES[route]
        step = 4 if d == 4 else -d
        arrive(("z", route, d), "z", step, (first, count), {"z": (shifted(pos, "z", d), 1)})

    def to_z(route, d):
        first, count, _, _ = ROUTES[route]
        step = 4 if d == 4 else -d
        push(("z", route, d), "z", step, (first, count), {})

    def to_middle(route, d):
        first, count, middle, _ = ROUTES[route]
        for m in NEAR:
            push(("m", route, d, m), middle, m, (first, count), {"z": (shifted(pos, "z", d), 1)})

    def from_middle(route, d):
        first, count, middle, _ = ROUTES[route]
        for m in NEAR:
            sel = {"z": (shifted(pos, "z", d), 1), middle: (shifted(pos, middle, -m), 1)}
            arrive(("m", route, d, m), middle, m, (first, count), sel)

    def to_last(route, d):
        first, count, middle, last = ROUTES[route]
        for way in (0, 1):
            sel = {"z": (shifted(pos, "z", d), 1), middle: full(middle)}
            push(("l", route, d, way), last, 1 - 2 * way, (first, count), sel)

    def pass_last(route, d):
        first, count, middle, last = ROUTES[route]
        for way in (0, 1):
            toward = 1 - 2 * way
            sel = {"z": (shifted(pos, "z", d), 1), middle: full(middle),
                   last: (shifted(pos, last, -toward), 1)}
            arrive(("l", route, d, way), last, toward, (first, count), sel)
            sel = dict(sel, **{middle: half(middle, way)})
            push(("p", route, d, way), last, toward, (first, count), sel)

    def from_last(route, d):
        first, count, middle, last = ROUTES[route]
        for way in (0, 1):
            toward = 1 - 2 * way
            sel = {"z": (shifted(pos, "z", d), 1), middle: half(middle, way),
                   last: (shifted(pos, last, -2 * toward), 1)}
            arrive(("p", route, d, way), last, toward, (first, count), sel)

    def ring_sel(part, step, way, arriving):
        toward = 1 - 2 * way
        back = step if arriving else step - 1
        sel = {"z": (shifted(pos, "z", -toward * back), 1), "y": half("y", part), "x": full("x")}
        if step == SIZES["z"] // 2:
            sel["x"] = half("x", way)
        return sel

    def a_ring(step):
        for part in (0, 1):
            for way in (0, 1):
                toward = 1 - 2 * way
                if step > 1:
                    arrive(("r", part, step - 1, way), "z", toward, ROUTE_A, ring_sel(part, step - 1, way, True))
                if step <= SIZES["z"] // 2:
                    push(("r", part, step, way), "z", toward, ROUTE_A, ring_sel(part, step, way, False))

    both = range(len(ROUTES))
    for m in NEAR:
        push(("y", m), "y", m, ROUTE_A, {})
    for group in GROUPS[1:]:
        for route in both:
            for d in group:
                to_z(route, d)
    for route in both:
        to_middle(route, 0)
    for m in NEAR:
        arrive(("y", m), "y", m, ROUTE_A, {"y": (shifted(pos, "y", -m), 1)})
    for m in NEAR:
        push(("x", m), "x", m, ROUTE_A, {"y": full("y")})
    for at in range(len(GROUPS) + 2):
        if at + 1 < len(GROUPS):
            for route in both:
                for d in GROUPS[at + 1]:
                    from_z(route, d)
                    to_middle(route, d)
        if at < len(GROUPS):
            for route in both:
                for d in GROUPS[at]:
                    from_middle(route, d)
                    to_last(route, d)
        if at == 0:
            for m in NEAR:
                arrive(("x", m), "x", m, ROUTE_A, {"y": full("y"), "x": (shifted(pos, "x", -m), 1)})
        if at <= SIZES["z"] // 2:
            a_ring(at + 1)
        if 0 < at <= len(GROUPS):
            for route in both:
                for d in GROUPS[at - 1]:
                    pass_last(route, d)
        if 1 < at:
            for route in both:
                for d in GROUPS[at - 2]:
                    from_last(route, d)
    for item in started:
        copy(*item).wait_send()
    for key, rows, sel in passed:
        side(key, core, rows, sel).wait_send()
        side(key, 1 - core, rows, sel).wait_recv()


def gather_all(keys, values):
    dims = tuple(SIZES[axis] for axis in AXES)
    sems = pltpu.SemaphoreType.DMA((COPIES,))
    anywhere = pl.BlockSpec(memory_space=pl.ANY)
    return pl.pallas_call(
        gather_kernel,
        out_shape=jax.ShapeDtypeStruct((2, *dims, ROWS, HD), jnp.bfloat16),
        in_specs=[anywhere, anywhere],
        out_specs=anywhere,
        scratch_shapes=[sems, sems, sems, sems, pltpu.SemaphoreType.DMA((2,))],
        compiler_params=pltpu.CompilerParams(collective_id=0, has_side_effects=True),
    )(keys.reshape(1, 1, 1, ROWS, HD), values.reshape(1, 1, 1, ROWS, HD))


def reduce_kernel(
    terms_ref, out_ref, held, other, final, ring_land, ax_land, ay_land, first_land, second_land,
    middle_land, z_land, send, recv, load_sem, side_send, side_recv, last_send, last_recv,
):
    pos, me, core = my_place()
    sibling = (me, 1 - core)

    def load(d):
        z = shifted(pos, "z", d)
        return pltpu.make_async_copy(terms_ref.at[core, z], held.at[z], load_sem.at[d % 8])

    def side(d):
        z = shifted(pos, "z", d)
        return pltpu.make_async_remote_copy(
            src_ref=terms_ref.at[1 - core, z], dst_ref=other.at[z],
            send_sem=side_send.at[d % 8], recv_sem=side_recv.at[d % 8],
            device_id=sibling, device_id_type=MESH,
        )

    far_first = GROUPS[::-1]
    for group in far_first:
        for d in group:
            load(d).start()
    greet(pos, me, core)
    for group in far_first:
        for d in group:
            side(d).start()

    number = Numbers()
    started = []

    def copy(key, axis, step, src, dst):
        at = number[key]
        return pltpu.make_async_remote_copy(
            src_ref=src, dst_ref=dst, send_sem=send.at[at], recv_sem=recv.at[at],
            device_id=peer(pos, core, axis, step), device_id_type=MESH,
        )

    def push(*item):
        copy(*item).start()
        started.append(item)

    def held_at(rows, **sel):
        index = []
        for axis in AXES:
            at = sel[axis] if axis in sel else pos[axis]
            index.append(pl.ds(*at) if isinstance(at, tuple) else at)
        return (*index, pl.ds(*rows), slice(None))

    def add(where, lands):
        total = as_f32(held[where])
        for land in lands:
            total = total + as_f32(land[...])
        held[where] = total.astype(jnp.bfloat16)

    def join(d):
        load(d).wait()
        side(d).wait_recv()
        z = shifted(pos, "z", d)

        def one(y, carry):
            for x in range(SIZES["x"]):
                held[z, y, x] = (as_f32(held[z, y, x]) + as_f32(other[z, y, x])).astype(jnp.bfloat16)
            return carry

        lax.fori_loop(0, SIZES["y"], one, 0)

    def middle_half(middle, way):
        size = SIZES[middle] // 2
        return (way * size, size)

    def first_copy(route, d, way):
        first, count, middle, last = ROUTES[route]
        where = {"z": shifted(pos, "z", d), middle: middle_half(middle, way), last: shifted(pos, last, 2)}
        return (("f", route, d, way), last, 1 - 2 * way, held.at[held_at((first, count), **where)],
                first_land.at[route, d % 8, way])

    def second_copy(route, d, way):
        first, count, middle, last = ROUTES[route]
        where = {"z": shifted(pos, "z", d), middle: (0, SIZES[middle]), last: shifted(pos, last, 1 - 2 * way)}
        return (("s", route, d, way), last, 1 - 2 * way, held.at[held_at((first, count), **where)],
                second_land.at[route, d % 8, way])

    def middle_copy(route, d, m):
        first, count, middle, last = ROUTES[route]
        where = {"z": shifted(pos, "z", d), middle: shifted(pos, middle, m)}
        return (("m", route, d, m), middle, m, held.at[held_at((first, count), **where)],
                middle_land.at[route, d % 8, NEAR.index(m)])

    def z_copy(route, d):
        first, count, _, _ = ROUTES[route]
        return (("z", route, d), "z", d, held.at[held_at((first, count), z=shifted(pos, "z", d))],
                z_land.at[route, Z_AWAY.index(d)])

    def send_first(route, d):
        for way in (0, 1):
            push(*first_copy(route, d, way))

    def send_second(route, d):
        first, count, middle, last = ROUTES[route]
        for way in (0, 1):
            copy(*first_copy(route, d, way)).wait_recv()
            low, size = middle_half(middle, way)
            for i in range(size):
                where = {"z": shifted(pos, "z", d), middle: low + i, last: shifted(pos, last, 1 - 2 * way)}
                add(held_at((first, count), **where), [first_land.at[route, d % 8, way, i]])
            push(*second_copy(route, d, way))

    def send_middle(route, d):
        first, count, middle, last = ROUTES[route]
        for way in (0, 1):
            copy(*second_copy(route, d, way)).wait_recv()
        for i in range(SIZES[middle]):
            where = {"z": shifted(pos, "z", d), middle: i}
            add(held_at((first, count), **where), [second_land.at[route, d % 8, way, i] for way in (0, 1)])
        for m in NEAR:
            push(*middle_copy(route, d, m))

    def send_z(route, d):
        first, count, _, _ = ROUTES[route]
        for m in NEAR:
            copy(*middle_copy(route, d, m)).wait_recv()
        where = held_at((first, count), z=shifted(pos, "z", d))
        add(where, [middle_land.at[route, d % 8, i] for i in range(len(NEAR))])
        if d != 0:
            push(*z_copy(route, d))

    def ring_copy(step, way):
        toward = 1 - 2 * way
        half = SIZES["x"] // 2
        xs = (way * half, half) if step == 1 else (0, SIZES["x"])
        where = {"z": shifted(pos, "z", toward * (5 - step)), "y": (0, SIZES["y"]), "x": xs}
        return (("r", step, way), "z", toward, held.at[held_at(ROUTE_A, **where)],
                ring_land.at[way, step - 1, :, pl.ds(*xs)])

    def ring(step):
        for way in (0, 1):
            toward = 1 - 2 * way
            half = SIZES["x"] // 2
            if 1 < step < 5:
                copy(*ring_copy(step - 1, way)).wait_recv()
                low, size = (way * half, half) if step == 2 else (0, SIZES["x"])
                z = shifted(pos, "z", toward * (5 - step))

                def one(y, carry):
                    for i in range(size):
                        add(held_at(ROUTE_A, z=z, y=y, x=low + i), [ring_land.at[way, step - 2, y, low + i]])
                    return carry

                lax.fori_loop(0, SIZES["y"], one, 0)
            if step < 5:
                push(*ring_copy(step, way))
        if step == 5:
            for way in (0, 1):
                copy(*ring_copy(4, way)).wait_recv()

            def last(y, carry):
                for x in range(SIZES["x"]):
                    add(held_at(ROUTE_A, y=y, x=x), [ring_land.at[way, 3, y, x] for way in (0, 1)])
                return carry

            lax.fori_loop(0, SIZES["y"], last, 0)

    def ax_copy(m):
        where = {"y": (0, SIZES["y"]), "x": shifted(pos, "x", m)}
        return (("ax", m), "x", m, held.at[held_at(ROUTE_A, **where)], ax_land.at[NEAR.index(m)])

    def ay_copy(m):
        where = {"y": shifted(pos, "y", m)}
        return (("ay", m), "y", m, held.at[held_at(ROUTE_A, **where)], ay_land.at[NEAR.index(m)])

    both = range(len(ROUTES))
    for at in range(len(far_first) + 3):
        if at < len(far_first):
            for d in far_first[at]:
                join(d)
            for route in both:
                for d in far_first[at]:
                    send_first(route, d)
            ring(at + 1)
        if at == len(far_first) - 1:
            for m in NEAR:
                push(*ax_copy(m))
        for behind, act in ((1, send_second), (2, send_middle), (3, send_z)):
            if 0 <= at - behind < len(far_first):
                for route in both:
                    for d in far_first[at - behind]:
                        act(route, d)
        if at == len(far_first):
            for m in NEAR:
                copy(*ax_copy(m)).wait_recv()
            for y in range(SIZES["y"]):
                add(held_at(ROUTE_A, y=y), [ax_land.at[i, y] for i in range(len(NEAR))])
            for m in NEAR:
                push(*ay_copy(m))
    for m in NEAR:
        copy(*ay_copy(m)).wait_recv()
    add(held_at(ROUTE_A), [ay_land.at[i] for i in range(len(NEAR))])
    for route in both:
        first, count, _, _ = ROUTES[route]
        for d in Z_AWAY:
            copy(*z_copy(route, d)).wait_recv()
        add(held_at((first, count)), [z_land.at[route, i] for i in range(len(Z_AWAY))])

    final[core] = held[pos["z"], pos["y"], pos["x"]]
    last_copy = pltpu.make_async_remote_copy(
        src_ref=final.at[core], dst_ref=final.at[core], send_sem=last_send, recv_sem=last_recv,
        device_id=sibling, device_id_type=MESH,
    )
    last_copy.start()
    for group in far_first:
        for d in group:
            side(d).wait_send()
    for item in started:
        copy(*item).wait_send()
    last_copy.wait()
    out_ref[...] = final[...]


def reduce_all(terms):
    dims = tuple(SIZES[axis] for axis in AXES)
    nz, ny, nx = dims

    def vmem(*shape):
        return pltpu.VMEM((*shape, HD), jnp.bfloat16)

    count = ROUTES[0][1]
    routes = len(ROUTES)
    sems = pltpu.SemaphoreType.DMA((COPIES,))
    by_z = pltpu.SemaphoreType.DMA((nz,))
    return pl.pallas_call(
        reduce_kernel,
        out_shape=jax.ShapeDtypeStruct((2, ROWS, HD), jnp.bfloat16),
        in_specs=[pl.BlockSpec(memory_space=pl.ANY)],
        out_specs=pl.BlockSpec(memory_space=pltpu.VMEM),
        scratch_shapes=[
            vmem(*dims, ROWS),
            vmem(*dims, ROWS),
            vmem(2, ROWS),
            vmem(2, nz // 2, ny, nx, ROUTE_A[1]),
            vmem(len(NEAR), ny, ROUTE_A[1]),
            vmem(len(NEAR), ROUTE_A[1]),
            vmem(routes, nz, 2, 2, count),
            vmem(routes, nz, 2, 4, count),
            vmem(routes, nz, len(NEAR), count),
            vmem(routes, len(Z_AWAY), count),
            sems, sems, by_z, by_z, by_z, pltpu.SemaphoreType.DMA, pltpu.SemaphoreType.DMA,
        ],
        compiler_params=pltpu.CompilerParams(
            collective_id=1, has_side_effects=True, vmem_limit_bytes=VMEM_BYTES
        ),
    )(terms)


def dot(left, right, contract):
    return lax.dot_general(
        left, right, ((contract[:1], contract[1:]), ((), ())), preferred_element_type=jnp.float32
    )


def attention_kernel(
    starts_ref, assign_ref, q_ref, g_ref, kv_ref, out_ref, dq_ref, terms_ref,
    place_ref, scores, probs, q_cols, g_cols, acc,
):
    heads = q_ref.shape[1] // HD
    cols = heads * SPAN
    scale = 1.0 / math.sqrt(HD)
    to_exp2 = scale * math.log2(math.e)
    per_block = BLOCK // SPAN

    def clear(at, carry):
        terms_ref[:, pl.ds(pl.multiple_of(at * 256, 256), 256), :] = jnp.zeros((2, 256, HD), jnp.bfloat16)
        return carry

    lax.fori_loop(0, terms_ref.shape[1] // 256, clear, 0)

    def locate(at, carry):
        for i in range(8):
            place_ref[assign_ref[at * 8 + i]] = at * 8 + i
        return carry

    lax.fori_loop(0, assign_ref.shape[0] // 8, locate, 0)
    first_span = lax.axis_index("ctx") * 2

    for part in range(2):
        base = assign_ref[first_span + part] * SPAN
        doc_first = jnp.int32(0)
        for doc in range(starts_ref.shape[0]):
            start = starts_ref[doc]
            doc_first = jnp.where(start <= base, jnp.maximum(doc_first, start), doc_first)
        first_block = doc_first // BLOCK
        full_blocks = base // BLOCK - first_block
        inside = base - (base // BLOCK) * BLOCK

        rows = pl.ds(part * SPAN, SPAN)
        q_rows = jnp.concatenate(
            [q_ref[rows, h * HD : (h + 1) * HD] for h in range(heads)], axis=0
        )
        g_rows = jnp.concatenate(
            [g_ref[rows, h * HD : (h + 1) * HD] for h in range(heads)], axis=0
        )
        q_t = as_f32(q_rows).T
        g_t = as_f32(g_rows).T
        q_cols[...] = q_t.astype(jnp.bfloat16)
        g_cols[...] = g_t.astype(jnp.bfloat16)

        def row_of(block, i):
            span = place_ref[(first_block + block) * per_block + i]
            return pl.ds(pl.multiple_of(span * SPAN, SPAN), SPAN)

        def tile(which, block):
            return jnp.concatenate(
                [kv_ref[which, row_of(block, i), :] for i in range(per_block)], axis=0
            )

        def fold(value, op):
            value = value.reshape(BLOCK // 8, 8, cols)
            return op(value, axis=0)

        def score_step(block, top):
            s = dot(tile(0, block), q_cols[...], (1, 0))
            scores[block] = s
            return jnp.maximum(top, fold(s, jnp.max))

        top = lax.fori_loop(0, full_blocks, score_step, jnp.full((8, cols), -1e30, jnp.float32))
        s = dot(tile(0, full_blocks), q_cols[...], (1, 0))
        key_at = lax.broadcasted_iota(jnp.int32, (BLOCK, cols), 0)
        query_at = lax.broadcasted_iota(jnp.int32, (BLOCK, cols), 1)
        s = jnp.where(key_at <= inside + lax.rem(query_at, SPAN), s, -1e30)
        scores[full_blocks] = s
        top = jnp.max(jnp.maximum(top, fold(s, jnp.max)), axis=0, keepdims=True)

        acc[...] = jnp.zeros_like(acc)

        def value_step(block, total):
            p = jnp.exp2((scores[block] - top) * to_exp2)
            p16 = p.astype(jnp.bfloat16)
            probs[block] = p16
            acc[...] += dot(tile(1, block), p16, (0, 0))
            return total + fold(p, jnp.sum)

        total = lax.fori_loop(0, full_blocks + 1, value_step, jnp.zeros((8, cols), jnp.float32))
        inverse = 1.0 / jnp.sum(total, axis=0, keepdims=True)
        out_t = (acc[...] * inverse).astype(jnp.bfloat16).astype(jnp.float32)
        delta = jnp.sum(g_t * out_t, axis=0, keepdims=True)
        q_scaled = (q_t * (inverse * scale)).astype(jnp.bfloat16)
        g_scaled = (g_t * inverse).astype(jnp.bfloat16)
        out_rows = out_t.T.astype(jnp.bfloat16)
        acc[...] = jnp.zeros_like(acc)

        def grad_step(block, carry):
            p16 = probs[block]
            keys = tile(0, block)
            d_probs = dot(tile(1, block), g_cols[...], (1, 0))
            d_scores = (as_f32(p16) * (d_probs - delta)).astype(jnp.bfloat16)
            acc[...] += dot(keys, d_scores, (0, 0))
            d_key = dot(d_scores, q_scaled, (1, 1))
            d_value = dot(p16, g_scaled, (1, 1))
            for i in range(per_block):
                at = row_of(block, i)
                for which, term in ((0, d_key), (1, d_value)):
                    piece = term[i * SPAN : (i + 1) * SPAN]
                    if part > 0:
                        piece = piece + as_f32(terms_ref[which, at, :])
                    terms_ref[which, at, :] = piece.astype(jnp.bfloat16)
            return carry

        lax.fori_loop(0, full_blocks + 1, grad_step, 0)
        dq_rows = (acc[...] * (inverse * scale)).T.astype(jnp.bfloat16)
        for h in range(heads):
            out_ref[rows, h * HD : (h + 1) * HD] = out_rows[h * SPAN : (h + 1) * SPAN]
            dq_ref[rows, h * HD : (h + 1) * HD] = dq_rows[h * SPAN : (h + 1) * SPAN]


def attention(doc_starts, assign, queries, d_out, kv_all):
    tokens = kv_all.shape[1]
    heads = queries.shape[1] // HD
    cols = heads * SPAN
    longest = tokens - (doc_starts.shape[0] - 1) * UNIT
    blocks = -(-longest // BLOCK)
    smem = pl.BlockSpec(memory_space=pltpu.SMEM)
    vmem = pl.BlockSpec(memory_space=pltpu.VMEM)
    return pl.pallas_call(
        attention_kernel,
        out_shape=(
            jax.ShapeDtypeStruct(queries.shape, jnp.bfloat16),
            jax.ShapeDtypeStruct(queries.shape, jnp.bfloat16),
            jax.ShapeDtypeStruct((2, tokens, HD), jnp.bfloat16),
        ),
        in_specs=[smem, smem, vmem, vmem, vmem],
        out_specs=(vmem, vmem, vmem),
        scratch_shapes=[
            pltpu.SMEM(assign.shape, jnp.int32),
            pltpu.VMEM((blocks, BLOCK, cols), jnp.float32),
            pltpu.VMEM((blocks, BLOCK, cols), jnp.bfloat16),
            pltpu.VMEM((HD, cols), jnp.bfloat16),
            pltpu.VMEM((HD, cols), jnp.bfloat16),
            pltpu.VMEM((HD, cols), jnp.float32),
        ],
        compiler_params=pltpu.CompilerParams(vmem_limit_bytes=VMEM_BYTES),
    )(doc_starts, assign, queries, d_out, kv_all)


def body(queries, keys, values, d_out, doc_starts, assign):
    tokens = assign.shape[0] * SPAN
    dims = tuple(SIZES[axis] for axis in AXES)
    kv_all = gather_all(keys, values).reshape(2, tokens, HD)
    attn_out, d_query, terms = attention(doc_starts, assign, queries, d_out, kv_all)
    summed = reduce_all(terms.reshape(2, *dims, ROWS, HD))
    return (attn_out, d_query, summed[0], summed[1])


def solution(mesh):
    placed = (P("ctx", "head"), P("ctx", None), P("ctx", None), P("ctx", "head"), P(), P())
    return jax.shard_map(
        body,
        mesh=mesh,
        in_specs=placed,
        out_specs=(P("ctx", "head"), P("ctx", "head"), P("ctx", None), P("ctx", None)),
        check_vma=False,
    )
```

time: 1330 us -> 114 us (0.09)
  waiting for transfers between devices: 786 us -> 0 us
  local copies, waits for them, and re-layouts: 366 us -> 1.4 us
  Pallas kernels: 0 us -> 112 us
  blocking collectives: 102 us -> 0 us
  other arithmetic: 33 us -> 0 us
  between operations: 20.9 us -> 0.65 us
  matrix products: 14.8 us -> 0 us
    reduce_scatter x1 -> x0, waiting for transfers between devices: 786 us -> none  [body(): lax.psum_scatter(stored_terms, 'ctx', scatter_dimension=0, tiled=True)]
    gather x4 -> x0, local copies, waits for them, and re-layouts: 336 us -> none  [the longest x1 101 us: body(): to_position = assign[positions // SPAN] * SPAN + positions % SPAN]
    pallas_call x0 -> x3, Pallas kernels: none -> 112 us  [the longest x1 49 us: gather_all(): pl.pallas_call(gather_kernel, out_shape=jax.ShapeDtypeStruct((2, *dims, R...]
    psum x1 -> x0, blocking collectives: 102 us -> none  [body(): summed = lax.psum(reduced, 'head').astype(jnp.bfloat16)]
    select_n x6 -> x0, other arithmetic: 20.5 us -> none  [the longest x2 12.3 us: body(): stored_terms = jnp.take(key_terms, to_position, axis=0)]
    while x3 -> x0, local copies, waits for them, and re-layouts: 17.5 us -> none  [the longest x1 17.5 us: span_pass(): lax.fori_loop(first_block, last_block, grad_step, start_grads)]
    dot_general x14 -> x0, matrix products: 14.8 us -> none  [the longest x6 7.85 us: contract_cols(): lax.dot_general(left, right, (((1,), (1,)), ((), ())), preferred_element_...]
  transfers between devices with their start and end apart: 2 -> 0, of which waited for: 1 -> 0; matrix products, arithmetic and copies ran while one was open for 16% -> 0% of each run, Pallas kernels for 0% -> 0%
where the time goes in v2:
time: 114 us
  Pallas kernels  112 us (98%)
  local copies, waits for them, and re-layouts  1.4 us (1%)
    pallas_call x1, Pallas kernels, gather_all(): pl.pallas_call(gather_kernel, out_shape=jax.ShapeDtypeStruct((2, *dims, R...  49 us
    pallas_call x1, Pallas kernels, reduce_all(): pl.pallas_call(reduce_kernel, out_shape=jax.ShapeDtypeStruct((2, ROWS, HD...  45.2 us
    pallas_call x1, Pallas kernels, attention(): pl.pallas_call(attention_kernel, out_shape=(jax.ShapeDtypeStruct(queries....  17.7 us

profile of v2, /device:TPU:1, one launch (start us, length us, event | category | flops | bytes accessed | tf_op | source)
XLA Modules:
  0.0 114.0 jit_solution(2689368490441461070)
XLA Ops:
  0.6 49.0 %shard_map.93 = bf16[2,8,4,4,128,128]{5,4,3,2,1,0:T(8,128)(2,1)} custom-call(bf16[1,1,1,128,128]{4,3,2,1,0:T(8,128)(2,1)} %bitcast.10, bf16[1,1,1,128,128]{4,3,2,1,0:T(8,128)(2,1)} %bitcast.11), custom_call_target="tpu_custom_call" | custom-call | tf_op jit(solution)/shard_map/pallas_call | solution.py:231
  49.7 17.7 %shard_map.94 = (bf16[128,1024]{1,0:T(8,128)(2,1)}, bf16[128,1024]{1,0:T(8,128)(2,1)}, bf16[2,16384,128]{2,1,0:T(8,128)(2,1)}) custom-call(s32[16]{0:T(128)} %starts_ref.1, s32[256]{0:T(256)} %assign_ref.1, bf16[128,1024]{1,0:T(8,128)(2,1)} %q_ref.1, bf16[128,1024]{1,0:T(8,128)(2,1)} %g_ref.1, bf16[2,16384,128]{2,1,0:T(8,128)(2,1)} %bitcast.8), custom_call_target="tpu_custom_call" | custom-call | tf_op jit(solution)/shard_map/pallas_call | solution.py:623
  67.3 45.2 %shard_map.95 = bf16[2,128,128]{2,1,0:T(8,128)(2,1)} custom-call(bf16[2,8,4,4,128,128]{5,4,3,2,1,0:T(8,128)(2,1)} %bitcast.9), custom_call_target="tpu_custom_call" | custom-call | tf_op jit(solution)/shard_map/pallas_call | solution.py:471
  112.6 1.4 %slice_bitcast_fusion = (bf16[128,128]{1,0:T(8,128)(2,1)}, bf16[128,128]{1,0:T(8,128)(2,1)}) fusion(bf16[2,128,128]{2,1,0:T(8,128)(2,1)} %shard_map.95), kind=kLoop, calls=%fused_computation | loop fusion | bytes 131072 | tf_op jit(solution)/shard_map/squeeze | solution.py:650

commit v3 on v2

v3 whole, which is shorter than its diff:
```python
import math

import jax
import jax.numpy as jnp
from jax import lax
from jax.experimental import pallas as pl
from jax.experimental.pallas import tpu as pltpu
from jax.sharding import PartitionSpec as P

HD = 128
SPAN = 64
ROWS = 2 * SPAN
BLOCK = 512
UNIT = 512
MESH = pl.DeviceIdType.MESH
AXES = ("z", "y", "x")
SIZES = {"z": 8, "y": 4, "x": 4}
ROUTE_A = (0, 32)
ROUTES = ((32, 48, "y", "x"), (80, 48, "x", "y"))
NEAR = (1, -1, 2)
Z_AWAY = (1, -1, 2, -2, 3, -3, 4)
GROUPS = ((0,), (1, -1), (2, -2), (3, -3), (4,))
DIRECT = (4,)
SUM_DIRECT = (0,)
COPIES = 80
ZERO_PIECES = 8
VMEM_BYTES = 60 * 1024 * 1024


def my_place():
    me = lax.axis_index("ctx")
    nx, ny = SIZES["x"], SIZES["y"]
    pos = {"x": lax.rem(me, nx), "y": lax.rem(me // nx, ny), "z": me // (nx * ny)}
    return pos, me, lax.axis_index("head")


def wrapped(value, size):
    return lax.rem(value + 2 * size, size)


def shifted(pos, axis, step):
    return wrapped(pos[axis] + step, SIZES[axis])


def peer(pos, core, axis, step):
    there = dict(pos)
    there[axis] = shifted(pos, axis, step)
    return ((there["z"] * SIZES["y"] + there["y"]) * SIZES["x"] + there["x"], core)


def greet(pos, me, core, along_z):
    barrier = pltpu.get_barrier_semaphore()
    partners = [("z", step) for step in along_z] + [(axis, step) for axis in "yx" for step in NEAR]
    for axis, step in partners:
        pl.semaphore_signal(
            barrier, inc=1, device_id=peer(pos, core, axis, step), device_id_type=MESH
        )
    pl.semaphore_signal(barrier, inc=1, device_id=(me, 1 - core), device_id_type=MESH)
    pl.semaphore_wait(barrier, len(partners) + 1)


def as_f32(value):
    return value.astype(jnp.float32)


class Numbers(dict):
    def __missing__(self, key):
        self[key] = len(self)
        assert len(self) <= COPIES
        return self[key]


def gather_kernel(
    k_ref, v_ref, all_ref, zeros_ref, recv, send_sem, side_send, side_recv, own_sem, zero_sem, blank
):
    pos, me, core = my_place()
    here = tuple(pl.ds(pos[axis], 1) for axis in AXES)
    for which, ref in ((0, k_ref), (1, v_ref)):
        @pl.when(core == which)
        def _(ref=ref):
            pltpu.make_async_copy(ref, all_ref.at[(core, *here)], own_sem).start()
    greet(pos, me, core, (1, -1))

    number = Numbers()
    sent_rows = []

    def view(owner, rows, **sel):
        index = [sel[axis] if axis in sel else (pos[axis], 1) for axis in AXES]
        return all_ref.at[(owner, *(pl.ds(*at) for at in index), pl.ds(*rows), slice(None))]

    def push(key, axis, step, rows, sel, src=None):
        ref = view(core, rows, **sel)
        pltpu.make_async_remote_copy(
            src_ref=ref if src is None else src.at[:, :, :, pl.ds(*rows), :],
            dst_ref=ref, send_sem=send_sem, recv_sem=recv.at[number[key]],
            device_id=peer(pos, core, axis, step), device_id_type=MESH,
        ).start()
        sent_rows.append(rows[1] * math.prod(count for _, count in sel.values()))

    def arrive(key, rows, sel):
        ref = view(core, rows, **sel)
        pltpu.make_async_remote_copy(
            src_ref=ref, dst_ref=ref, send_sem=send_sem, recv_sem=recv.at[number[key]],
            device_id=(me, 1 - core), device_id_type=MESH,
        ).wait_recv()

    def side(ref):
        return pltpu.make_async_remote_copy(
            src_ref=ref, dst_ref=ref, send_sem=side_send, recv_sem=side_recv,
            device_id=(me, 1 - core), device_id_type=MESH,
        )

    def hand_over(rows, **sel):
        side(view(core, rows, **sel)).start()

    def full(axis):
        return (0, SIZES[axis])

    def half(axis, side_at):
        return (side_at * (SIZES[axis] // 2), SIZES[axis] // 2)

    def z_way(route, d):
        if d == 4:
            return 1 - 2 * route
        return -1 if d > 0 else 1

    def at_z(d):
        return (shifted(pos, "z", d), 1)

    def to_z(route, d, src=None):
        first, count, _, _ = ROUTES[route]
        toward = z_way(route, d)
        push(("z", route, d), "z", toward, (first, count), {"z": at_z(d + toward)}, src)

    def from_z(route, d):
        first, count, _, _ = ROUTES[route]
        arrive(("z", route, d), (first, count), {"z": at_z(d)})
        if abs(d) < 3:
            to_z(route, d - z_way(route, d))
        elif d != 4 and z_way(route, d) == z_way(route, 4):
            to_z(route, 4)

    def to_middle(route, d, src=None):
        first, count, middle, _ = ROUTES[route]
        for m in NEAR:
            push(("m", route, d), middle, m, (first, count), {"z": at_z(d)}, src)

    def from_middle(route, d):
        first, count, middle, _ = ROUTES[route]
        arrive(("m", route, d), (first, count), {"z": at_z(d), middle: (0, len(NEAR))})

    def to_last(route, d):
        first, count, middle, last = ROUTES[route]
        sel = {"z": at_z(d), middle: full(middle)}
        for m in (NEAR if d in DIRECT else NEAR[:2]):
            push(("l", route, d), last, m, (first, count), sel)

    def whole_plane(route, d):
        first, count, _, _ = ROUTES[route]
        hand_over((first, count), z=at_z(d), y=full("y"), x=full("x"))

    def pass_last(route, d):
        first, count, middle, last = ROUTES[route]
        copies = len(NEAR) if d in DIRECT else 2
        arrive(("l", route, d), (first, count), {"z": at_z(d), middle: full(middle), last: (0, copies)})
        if d in DIRECT:
            whole_plane(route, d)
            return
        for way, m in enumerate(NEAR[:2]):
            sel = {"z": at_z(d), middle: half(middle, way), last: (shifted(pos, last, -m), 1)}
            push(("p", route, d), last, m, (first, count), sel)

    def from_last(route, d):
        first, count, middle, last = ROUTES[route]
        if d in DIRECT:
            return
        arrive(("p", route, d), (first, count), {"z": at_z(d), middle: full(middle)})
        whole_plane(route, d)

    def ring_sel(part, step, way, arriving):
        toward = 1 - 2 * way
        back = step if arriving else step - 1
        sel = {"z": (shifted(pos, "z", -toward * back), 1), "y": half("y", part), "x": full("x")}
        if step == SIZES["z"] // 2:
            sel["x"] = half("x", way)
        return sel

    def a_ring(step):
        steps = SIZES["z"] // 2
        for part in (0, 1):
            for way in (0, 1):
                if step > 1:
                    arrive(("r", part, step - 1, way), ROUTE_A, ring_sel(part, step - 1, way, True))
                if step <= steps:
                    push(("r", part, step, way), "z", 1 - 2 * way, ROUTE_A, ring_sel(part, step, way, False))
        for d in {1: (0,), steps + 1: (steps,)}.get(step, (step - 1, 1 - step)):
            hand_over(ROUTE_A, z=at_z(d), y=full("y"), x=full("x"))

    both = range(len(ROUTES))

    def begin(src):
        for route in both:
            for d in GROUPS[1]:
                to_z(route, d, src)
        for route in both:
            to_middle(route, 0, src)
        for m in NEAR:
            push(("y",), "y", m, ROUTE_A, {}, src)

    for which, ref in ((0, k_ref), (1, v_ref)):
        @pl.when(core == which)
        def _(ref=ref):
            sent_rows.clear()
            begin(ref)
    pltpu.make_async_copy(k_ref, all_ref.at[(core, *here)], own_sem).wait()
    blank[...] = jnp.zeros_like(blank)
    piece = blank.shape[0]
    pieces = zeros_ref.shape[0] // piece

    def wipe(at):
        return pltpu.make_async_copy(blank, zeros_ref.at[pl.ds(at * piece, piece)], zero_sem.at[at])

    for at in range(len(GROUPS) + 2):
        if at + 1 < len(GROUPS):
            for route in both:
                for d in GROUPS[at + 1]:
                    from_z(route, d)
                    to_middle(route, d)
        if at < len(GROUPS):
            for route in both:
                for d in GROUPS[at]:
                    from_middle(route, d)
                    to_last(route, d)
        if at == 0:
            arrive(("y",), ROUTE_A, {"y": (0, len(NEAR))})
            for m in NEAR:
                push(("x",), "x", m, ROUTE_A, {"y": full("y")})
        if at == 1:
            arrive(("x",), ROUTE_A, {"y": full("y"), "x": (0, len(NEAR))})
        if 0 < at <= SIZES["z"] // 2 + 1:
            a_ring(at)
        if 0 < at <= len(GROUPS):
            for route in both:
                for d in GROUPS[at - 1]:
                    pass_last(route, d)
        if 1 < at:
            for route in both:
                for d in GROUPS[at - 2]:
                    from_last(route, d)
        for i in range(at * 2, min(at * 2 + 2, pieces)):
            wipe(i).start()
    for at in range(pieces):
        wipe(at).wait()
    sent = zeros_ref.at[pl.ds(0, sum(sent_rows))]
    pltpu.make_async_remote_copy(
        src_ref=sent, dst_ref=sent, send_sem=send_sem, recv_sem=side_recv,
        device_id=(me, 1 - core), device_id_type=MESH,
    ).wait_send()
    side(all_ref.at[core]).wait_send()
    side(all_ref.at[1 - core]).wait_recv()


def gather_all(keys, values):
    dims = tuple(SIZES[axis] for axis in AXES)
    sems = pltpu.SemaphoreType.DMA((COPIES,))
    one_sem = pltpu.SemaphoreType.DMA
    piece = 2 * math.prod(dims) * ROWS // ZERO_PIECES
    anywhere = pl.BlockSpec(memory_space=pl.ANY)
    return pl.pallas_call(
        gather_kernel,
        out_shape=(
            jax.ShapeDtypeStruct((2, *dims, ROWS, HD), jnp.bfloat16),
            jax.ShapeDtypeStruct((ZERO_PIECES * piece, HD), jnp.bfloat16),
        ),
        in_specs=[anywhere, anywhere],
        out_specs=(anywhere, anywhere),
        scratch_shapes=[sems, one_sem, one_sem, one_sem, one_sem,
                        pltpu.SemaphoreType.DMA((ZERO_PIECES,)), pltpu.VMEM((piece, HD), jnp.bfloat16)],
        compiler_params=pltpu.CompilerParams(
            collective_id=0, has_side_effects=True, vmem_limit_bytes=VMEM_BYTES
        ),
    )(keys.reshape(1, 1, 1, ROWS, HD), values.reshape(1, 1, 1, ROWS, HD))


def reduce_kernel(
    terms_ref, out_ref, held, other, final, ring_land, ax_land, ay_land, first_land, second_land,
    direct_land, middle_land, z_land, send, recv, load_sem, side_send, side_recv, last_send, last_recv,
):
    pos, me, core = my_place()
    sibling = (me, 1 - core)

    def load(d):
        z = shifted(pos, "z", d)
        return pltpu.make_async_copy(terms_ref.at[core, z], held.at[z], load_sem.at[d % 8])

    def side(d):
        z = shifted(pos, "z", d)
        return pltpu.make_async_remote_copy(
            src_ref=terms_ref.at[1 - core, z], dst_ref=other.at[z],
            send_sem=side_send, recv_sem=side_recv.at[d % 8],
            device_id=sibling, device_id_type=MESH,
        )

    far_first = GROUPS[::-1]
    for group in far_first:
        for d in group:
            load(d).start()
    greet(pos, me, core, Z_AWAY)
    for group in far_first:
        for d in group:
            side(d).start()

    number, kind = Numbers(), Numbers()

    def copy(key, axis, step, src, dst):
        return pltpu.make_async_remote_copy(
            src_ref=src, dst_ref=dst, send_sem=send.at[kind[key[0]]], recv_sem=recv.at[number[key]],
            device_id=peer(pos, core, axis, step), device_id_type=MESH,
        )

    def push(*item):
        copy(*item).start()

    def arrived(key, land):
        copy(key, "z", 1, land, land).wait_recv()

    def left(name, land):
        copy((name,), "z", 1, land, land).wait_send()

    def held_at(rows, **sel):
        index = []
        for axis in AXES:
            at = sel[axis] if axis in sel else pos[axis]
            index.append(pl.ds(*at) if isinstance(at, tuple) else at)
        return (*index, pl.ds(*rows), slice(None))

    def add(where, lands):
        total = as_f32(held[where])
        for land in lands:
            total = total + as_f32(land[...])
        held[where] = total.astype(jnp.bfloat16)

    def join(d):
        load(d).wait()
        side(d).wait_recv()
        z = shifted(pos, "z", d)

        def one(y, carry):
            for x in range(SIZES["x"]):
                held[z, y, x] = (as_f32(held[z, y, x]) + as_f32(other[z, y, x])).astype(jnp.bfloat16)
            return carry

        lax.fori_loop(0, SIZES["y"], one, 0)

    def middle_half(middle, way):
        size = SIZES[middle] // 2
        return (way * size, size)

    def first_copy(route, d, way):
        first, count, middle, last = ROUTES[route]
        where = {"z": shifted(pos, "z", d), middle: middle_half(middle, way), last: shifted(pos, last, 2)}
        return (("f", route, d), last, 1 - 2 * way, held.at[held_at((first, count), **where)],
                first_land.at[route, d % 8, way])

    def second_copy(route, d, way):
        first, count, middle, last = ROUTES[route]
        where = {"z": shifted(pos, "z", d), middle: (0, SIZES[middle]), last: shifted(pos, last, 1 - 2 * way)}
        return (("s", route, d), last, 1 - 2 * way, held.at[held_at((first, count), **where)],
                second_land.at[route, d % 8, way])

    def middle_copy(route, d, m):
        first, count, middle, last = ROUTES[route]
        where = {"z": shifted(pos, "z", d), middle: shifted(pos, middle, m)}
        return (("m", route, d), middle, m, held.at[held_at((first, count), **where)],
                middle_land.at[route, d % 8, NEAR.index(m)])

    def z_copy(route, d):
        first, count, _, _ = ROUTES[route]
        return (("z", route), "z", d, held.at[held_at((first, count), z=shifted(pos, "z", d))],
                z_land.at[route, Z_AWAY.index(d)])

    def direct_copy(route, d, m):
        first, count, middle, last = ROUTES[route]
        where = {"z": shifted(pos, "z", d), middle: (0, SIZES[middle]), last: shifted(pos, last, m)}
        return (("d", route, d), last, m, held.at[held_at((first, count), **where)],
                direct_land.at[route, SUM_DIRECT.index(d), NEAR.index(m)])

    def send_first(route, d):
        if d in SUM_DIRECT:
            for m in NEAR:
                push(*direct_copy(route, d, m))
            return
        for way in (0, 1):
            push(*first_copy(route, d, way))

    def send_second(route, d):
        first, count, middle, last = ROUTES[route]
        arrived(("f", route, d), first_land.at[route, d % 8])
        for way in (0, 1):
            low, size = middle_half(middle, way)
            for i in range(size):
                where = {"z": shifted(pos, "z", d), middle: low + i, last: shifted(pos, last, 1 - 2 * way)}
                add(held_at((first, count), **where), [first_land.at[route, d % 8, way, i]])
            push(*second_copy(route, d, way))

    def send_middle(route, d):
        first, count, middle, last = ROUTES[route]
        if d in SUM_DIRECT:
            arrived(("d", route, d), direct_land.at[route, SUM_DIRECT.index(d)])
            lands = [direct_land.at[route, SUM_DIRECT.index(d), i] for i in range(len(NEAR))]
        else:
            arrived(("s", route, d), second_land.at[route, d % 8])
            lands = [second_land.at[route, d % 8, way] for way in (0, 1)]
        for i in range(SIZES[middle]):
            where = {"z": shifted(pos, "z", d), middle: i}
            add(held_at((first, count), **where), [land.at[i] for land in lands])
        for m in NEAR:
            push(*middle_copy(route, d, m))

    def send_z(route, d):
        first, count, _, _ = ROUTES[route]
        arrived(("m", route, d), middle_land.at[route, d % 8])
        where = held_at((first, count), z=shifted(pos, "z", d))
        add(where, [middle_land.at[route, d % 8, i] for i in range(len(NEAR))])
        if d != 0:
            push(*z_copy(route, d))

    def ring_copy(step, way):
        toward = 1 - 2 * way
        half = SIZES["x"] // 2
        xs = (way * half, half) if step == 1 else (0, SIZES["x"])
        where = {"z": shifted(pos, "z", toward * (5 - step)), "y": (0, SIZES["y"]), "x": xs}
        return (("h" if step == 1 else "r", step, way), "z", toward, held.at[held_at(ROUTE_A, **where)],
                ring_land.at[way, step - 1, :, pl.ds(*xs)])

    def ring(step):
        for way in (0, 1):
            toward = 1 - 2 * way
            half = SIZES["x"] // 2
            if 1 < step < 5:
                copy(*ring_copy(step - 1, way)).wait_recv()
                low, size = (way * half, half) if step == 2 else (0, SIZES["x"])
                z = shifted(pos, "z", toward * (5 - step))

                def one(y, carry):
                    for i in range(size):
                        add(held_at(ROUTE_A, z=z, y=y, x=low + i), [ring_land.at[way, step - 2, y, low + i]])
                    return carry

                lax.fori_loop(0, SIZES["y"], one, 0)
            if step < 5:
                push(*ring_copy(step, way))
        if step == 5:
            for way in (0, 1):
                copy(*ring_copy(4, way)).wait_recv()

            def last(y, carry):
                for x in range(SIZES["x"]):
                    add(held_at(ROUTE_A, y=y, x=x), [ring_land.at[way, 3, y, x] for way in (0, 1)])
                return carry

            lax.fori_loop(0, SIZES["y"], last, 0)

    def ax_copy(m):
        where = {"y": (0, SIZES["y"]), "x": shifted(pos, "x", m)}
        return (("ax",), "x", m, held.at[held_at(ROUTE_A, **where)], ax_land.at[NEAR.index(m)])

    def ay_copy(m):
        where = {"y": shifted(pos, "y", m)}
        return (("ay",), "y", m, held.at[held_at(ROUTE_A, **where)], ay_land.at[NEAR.index(m)])

    both = range(len(ROUTES))
    for at in range(len(far_first) + 2):
        if at < len(far_first):
            for d in far_first[at]:
                join(d)
            for route in both:
                for d in far_first[at]:
                    send_first(route, d)
            ring(at + 1)
        if at == len(far_first) - 1:
            for m in NEAR:
                push(*ax_copy(m))
        for behind, act in ((1, send_second), (2, send_middle), (3, send_z)):
            for begun, group in enumerate(far_first):
                for d in group:
                    sooner = 1 if d in SUM_DIRECT else 0
                    if begun + behind - sooner == at and not (sooner and act is send_second):
                        for route in both:
                            act(route, d)
        if at == len(far_first):
            arrived(("ax",), ax_land)
            for y in range(SIZES["y"]):
                add(held_at(ROUTE_A, y=y), [ax_land.at[i, y] for i in range(len(NEAR))])
            for m in NEAR:
                push(*ay_copy(m))
    arrived(("ay",), ay_land)
    add(held_at(ROUTE_A), [ay_land.at[i] for i in range(len(NEAR))])
    for route in both:
        first, count, _, _ = ROUTES[route]
        arrived(("z", route), z_land.at[route])
        add(held_at((first, count)), [z_land.at[route, i] for i in range(len(Z_AWAY))])

    final[core] = held[pos["z"], pos["y"], pos["x"]]
    last_copy = pltpu.make_async_remote_copy(
        src_ref=final.at[core], dst_ref=final.at[core], send_sem=last_send, recv_sem=last_recv,
        device_id=sibling, device_id_type=MESH,
    )
    last_copy.start()
    pltpu.make_async_remote_copy(
        src_ref=other, dst_ref=other, send_sem=side_send, recv_sem=last_recv,
        device_id=sibling, device_id_type=MESH,
    ).wait_send()
    relayed = pl.ds(0, SIZES["z"] - len(SUM_DIRECT))
    left("f", first_land.at[:, relayed])
    left("s", second_land.at[:, relayed])
    left("d", direct_land)
    left("m", middle_land)
    left("z", z_land)
    left("h", ring_land.at[:, 0, :, pl.ds(0, SIZES["x"] // 2)])
    left("r", ring_land.at[:, pl.ds(1, 3)])
    left("ax", ax_land)
    left("ay", ay_land)
    last_copy.wait()
    out_ref[...] = final[...]


def reduce_all(terms):
    dims = tuple(SIZES[axis] for axis in AXES)
    nz, ny, nx = dims

    def vmem(*shape):
        return pltpu.VMEM((*shape, HD), jnp.bfloat16)

    count = ROUTES[0][1]
    routes = len(ROUTES)
    sems = pltpu.SemaphoreType.DMA((COPIES,))
    by_z = pltpu.SemaphoreType.DMA((nz,))
    one_sem = pltpu.SemaphoreType.DMA
    return pl.pallas_call(
        reduce_kernel,
        out_shape=jax.ShapeDtypeStruct((2, ROWS, HD), jnp.bfloat16),
        in_specs=[pl.BlockSpec(memory_space=pl.ANY)],
        out_specs=pl.BlockSpec(memory_space=pltpu.VMEM),
        scratch_shapes=[
            vmem(*dims, ROWS),
            vmem(*dims, ROWS),
            vmem(2, ROWS),
            vmem(2, nz // 2, ny, nx, ROUTE_A[1]),
            vmem(len(NEAR), ny, ROUTE_A[1]),
            vmem(len(NEAR), ROUTE_A[1]),
            vmem(routes, nz, 2, 2, count),
            vmem(routes, nz, 2, 4, count),
            vmem(routes, len(SUM_DIRECT), len(NEAR), 4, count),
            vmem(routes, nz, len(NEAR), count),
            vmem(routes, len(Z_AWAY), count),
            pltpu.SemaphoreType.DMA((9,)), sems, by_z, one_sem, by_z, one_sem, one_sem,
        ],
        compiler_params=pltpu.CompilerParams(
            collective_id=1, has_side_effects=True, vmem_limit_bytes=VMEM_BYTES
        ),
    )(terms)


def dot(left, right, contract):
    return lax.dot_general(
        left, right, ((contract[:1], contract[1:]), ((), ())), preferred_element_type=jnp.float32
    )


def attention_kernel(
    starts_ref, assign_ref, q_ref, g_ref, kv_ref, zeros_ref, out_ref, dq_ref, terms_ref,
    place_ref, tiles, sums, scores, probs, q_cols, g_cols, acc, in_sem, out_sem,
):
    del zeros_ref
    heads = q_ref.shape[1] // HD
    cols = heads * SPAN
    scale = 1.0 / math.sqrt(HD)
    to_exp2 = scale * math.log2(math.e)
    per_block = BLOCK // SPAN

    def locate(at, carry):
        for i in range(16):
            place_ref[assign_ref[at * 16 + i]] = at * 16 + i
        return carry

    lax.fori_loop(0, assign_ref.shape[0] // 16, locate, 0)
    first_span = lax.axis_index("ctx") * 2
    bases, firsts, lasts = [], [], []
    for part in range(2):
        base = assign_ref[first_span + part] * SPAN
        doc_first = jnp.int32(0)
        for doc in range(starts_ref.shape[0]):
            start = starts_ref[doc]
            doc_first = jnp.where(start <= base, jnp.maximum(doc_first, start), doc_first)
        bases.append(base)
        firsts.append(doc_first // BLOCK)
        lasts.append(base // BLOCK)

    def rows_at(at, count):
        return pl.ds(pl.multiple_of(at * count, count), count)

    def stored(block, i):
        return rows_at(place_ref[block * per_block + i], SPAN)

    def fetch(part, at):
        for i in range(per_block):
            pltpu.make_async_copy(
                kv_ref.at[:, stored(firsts[part] + at, i), :],
                tiles.at[part, :, rows_at(at * per_block + i, SPAN), :],
                in_sem.at[part, at],
            ).start()

    def fetched(part, at):
        pltpu.make_async_copy(
            kv_ref.at[:, pl.ds(0, BLOCK), :], tiles.at[part, :, rows_at(at, BLOCK), :], in_sem.at[part, at]
        ).wait()

    def store(block):
        for i in range(per_block):
            pltpu.make_async_copy(
                sums.at[:, rows_at(block * per_block + i, SPAN), :],
                terms_ref.at[:, stored(block, i), :],
                out_sem.at[block],
            ).start()

    def stored_all(block):
        pltpu.make_async_copy(
            sums.at[:, rows_at(block, BLOCK), :], terms_ref.at[:, pl.ds(0, BLOCK), :], out_sem.at[block]
        ).wait()

    def shared(block):
        return (block >= firsts[1]) & (block <= lasts[1])

    for part in range(2):
        lax.fori_loop(0, lasts[part] - firsts[part] + 1, lambda at, c, part=part: (fetch(part, at), c)[1], 0)

    for part in range(2):
        base = bases[part]
        full_blocks = lasts[part] - firsts[part]
        inside = base - lasts[part] * BLOCK

        rows = pl.ds(part * SPAN, SPAN)
        q_rows = jnp.concatenate(
            [q_ref[rows, h * HD : (h + 1) * HD] for h in range(heads)], axis=0
        )
        g_rows = jnp.concatenate(
            [g_ref[rows, h * HD : (h + 1) * HD] for h in range(heads)], axis=0
        )
        q_t = as_f32(q_rows).T
        g_t = as_f32(g_rows).T
        q_cols[...] = q_t.astype(jnp.bfloat16)
        g_cols[...] = g_t.astype(jnp.bfloat16)

        def tile(which, at, part=part):
            return tiles[part, which, rows_at(at, BLOCK), :]

        def fold(value, op):
            value = value.reshape(BLOCK // 8, 8, cols)
            return op(value, axis=0)

        def score_step(at, top, part=part):
            fetched(part, at)
            s = dot(tile(0, at), q_cols[...], (1, 0))
            scores[at] = s
            return jnp.maximum(top, fold(s, jnp.max))

        top = lax.fori_loop(0, full_blocks, score_step, jnp.full((8, cols), -1e30, jnp.float32))
        fetched(part, full_blocks)
        s = dot(tile(0, full_blocks), q_cols[...], (1, 0))
        key_at = lax.broadcasted_iota(jnp.int32, (BLOCK, cols), 0)
        query_at = lax.broadcasted_iota(jnp.int32, (BLOCK, cols), 1)
        s = jnp.where(key_at <= inside + lax.rem(query_at, SPAN), s, -1e30)
        scores[full_blocks] = s
        top = jnp.max(jnp.maximum(top, fold(s, jnp.max)), axis=0, keepdims=True)

        acc[...] = jnp.zeros_like(acc)

        def value_step(at, total):
            p = jnp.exp2((scores[at] - top) * to_exp2)
            p16 = p.astype(jnp.bfloat16)
            probs[at] = p16
            acc[...] += dot(tile(1, at), p16, (0, 0))
            return total + fold(p, jnp.sum)

        total = lax.fori_loop(0, full_blocks + 1, value_step, jnp.zeros((8, cols), jnp.float32))
        inverse = 1.0 / jnp.sum(total, axis=0, keepdims=True)
        out_t = (acc[...] * inverse).astype(jnp.bfloat16).astype(jnp.float32)
        delta = jnp.sum(g_t * out_t, axis=0, keepdims=True)
        q_scaled = (q_t * (inverse * scale)).astype(jnp.bfloat16)
        g_scaled = (g_t * inverse).astype(jnp.bfloat16)
        out_rows = out_t.T.astype(jnp.bfloat16)
        acc[...] = jnp.zeros_like(acc)

        def grad_step(at, carry, part=part):
            block = firsts[part] + at
            p16 = probs[at]
            keys = tile(0, at)
            d_probs = dot(tile(1, at), g_cols[...], (1, 0))
            d_scores = (as_f32(p16) * (d_probs - delta)).astype(jnp.bfloat16)
            acc[...] += dot(keys, d_scores, (0, 0))
            d_key = dot(d_scores, q_scaled, (1, 1))
            d_value = dot(p16, g_scaled, (1, 1))
            here = rows_at(block, BLOCK)
            for which, term in ((0, d_key), (1, d_value)):
                if part > 0:
                    both = (block >= firsts[0]) & (block <= lasts[0])
                    term = term + jnp.where(both, as_f32(sums[which, here, :]), 0.0)
                sums[which, here, :] = term.astype(jnp.bfloat16)
            if part > 0:
                store(block)
            else:
                pl.when(jnp.logical_not(shared(block)))(lambda: store(block))
            return carry

        lax.fori_loop(0, full_blocks + 1, grad_step, 0)
        dq_rows = (acc[...] * (inverse * scale)).T.astype(jnp.bfloat16)
        for h in range(heads):
            out_ref[rows, h * HD : (h + 1) * HD] = out_rows[h * SPAN : (h + 1) * SPAN]
            dq_ref[rows, h * HD : (h + 1) * HD] = dq_rows[h * SPAN : (h + 1) * SPAN]

    def drain(block, carry, part):
        if part > 0:
            stored_all(block)
        else:
            pl.when(jnp.logical_not(shared(block)))(lambda: stored_all(block))
        return carry

    for part in range(2):
        lax.fori_loop(firsts[part], lasts[part] + 1, lambda block, c, part=part: drain(block, c, part), 0)


def attention(doc_starts, assign, queries, d_out, kv_all, zeros):
    tokens = kv_all.shape[1]
    heads = queries.shape[1] // HD
    cols = heads * SPAN
    longest = tokens - (doc_starts.shape[0] - 1) * UNIT
    blocks = -(-longest // BLOCK)
    smem = pl.BlockSpec(memory_space=pltpu.SMEM)
    vmem = pl.BlockSpec(memory_space=pltpu.VMEM)
    anywhere = pl.BlockSpec(memory_space=pl.ANY)
    return pl.pallas_call(
        attention_kernel,
        out_shape=(
            jax.ShapeDtypeStruct(queries.shape, jnp.bfloat16),
            jax.ShapeDtypeStruct(queries.shape, jnp.bfloat16),
            jax.ShapeDtypeStruct(zeros.shape, jnp.bfloat16),
        ),
        in_specs=[smem, smem, vmem, vmem, anywhere, anywhere],
        out_specs=(vmem, vmem, anywhere),
        input_output_aliases={5: 2},
        scratch_shapes=[
            pltpu.SMEM(assign.shape, jnp.int32),
            pltpu.VMEM((2, 2, blocks * BLOCK, HD), jnp.bfloat16),
            pltpu.VMEM((2, tokens, HD), jnp.bfloat16),
            pltpu.VMEM((blocks, BLOCK, cols), jnp.float32),
            pltpu.VMEM((blocks, BLOCK, cols), jnp.bfloat16),
            pltpu.VMEM((HD, cols), jnp.bfloat16),
            pltpu.VMEM((HD, cols), jnp.bfloat16),
            pltpu.VMEM((HD, cols), jnp.float32),
            pltpu.SemaphoreType.DMA((2, blocks)),
            pltpu.SemaphoreType.DMA((tokens // BLOCK,)),
        ],
        compiler_params=pltpu.CompilerParams(vmem_limit_bytes=VMEM_BYTES),
    )(doc_starts, assign, queries, d_out, kv_all, zeros)


def body(queries, keys, values, d_out, doc_starts, assign):
    tokens = assign.shape[0] * SPAN
    dims = tuple(SIZES[axis] for axis in AXES)
    kv_all, zeros = gather_all(keys, values)
    attn_out, d_query, terms = attention(
        doc_starts, assign, queries, d_out, kv_all.reshape(2, tokens, HD), zeros.reshape(2, tokens, HD)
    )
    summed = reduce_all(terms.reshape(2, *dims, ROWS, HD))
    return (attn_out, d_query, summed[0], summed[1])


def solution(mesh):
    placed = (P("ctx", "head"), P("ctx", None), P("ctx", None), P("ctx", "head"), P(), P())
    return jax.shard_map(
        body,
        mesh=mesh,
        in_specs=placed,
        out_specs=(P("ctx", "head"), P("ctx", "head"), P("ctx", None), P("ctx", None)),
        check_vma=False,
    )
```

time: 114 us -> 94.8 us (0.83)
  Pallas kernels: 112 us -> 92.5 us
    pallas_call x1, Pallas kernels: 17.7 us -> 7.73 us  [attention(): pl.pallas_call(attention_kernel, out_shape=(jax.ShapeDtypeStruct(queries....]
    pallas_call x1, Pallas kernels: 49 us -> 40.7 us  [gather_all(): pl.pallas_call(gather_kernel, out_shape=(jax.ShapeDtypeStruct((2, *dims,...]
    pallas_call x1, Pallas kernels: 45.2 us -> 44.1 us  [reduce_all(): pl.pallas_call(reduce_kernel, out_shape=jax.ShapeDtypeStruct((2, ROWS, HD...]
where the time goes in v3:
time: 94.8 us; the launch traced here: 94.6 us
  Pallas kernels  92.5 us (98%)
  local copies, waits for them, and re-layouts  1.4 us (1%)
    pallas_call x1, Pallas kernels, reduce_all(): pl.pallas_call(reduce_kernel, out_shape=jax.ShapeDtypeStruct((2, ROWS, HD...  44.1 us
    pallas_call x1, Pallas kernels, gather_all(): pl.pallas_call(gather_kernel, out_shape=(jax.ShapeDtypeStruct((2, *dims,...  40.7 us
    pallas_call x1, Pallas kernels, attention(): pl.pallas_call(attention_kernel, out_shape=(jax.ShapeDtypeStruct(queries....  7.73 us

profile of v3, /device:TPU:1, one launch (start us, length us, event | category | flops | bytes accessed | tf_op | source)
XLA Modules:
  0.0 94.6 jit_solution(3876954291679757443)
XLA Ops:
  0.6 40.7 %shard_map.93 = (bf16[2,8,4,4,128,128]{5,4,3,2,1,0:T(8,128)(2,1)}, bf16[32768,128]{1,0:T(8,128)(2,1)}) custom-call(bf16[1,1,1,128,128]{4,3,2,1,0:T(8,128)(2,1)} %bitcast.12, bf16[1,1,1,128,128]{4,3,2,1,0:T(8,128)(2,1)} %bitcast.13), custom_call_target="tpu_custom_call" | custom-call | tf_op jit(solution)/shard_map/pallas_call | solution.py:269
  41.4 7.7 %shard_map.94 = (bf16[128,1024]{1,0:T(8,128)(2,1)}, bf16[128,1024]{1,0:T(8,128)(2,1)}, bf16[2,16384,128]{2,1,0:T(8,128)(2,1)}) custom-call(s32[16]{0:T(128)} %starts_ref.1, s32[256]{0:T(256)} %assign_ref.1, bf16[128,1024]{1,0:T(8,128)(2,1)} %q_ref.1, bf16[128,1024]{1,0:T(8,128)(2,1)} %g_ref.1, ...), custom_call_target="tpu_custom_call", output_to_operand_aliasing={{2}: (5, {})} | custom-call | tf_op jit(solution)/shard_map/pallas_call | solution.py:742
  49.1 44.1 %shard_map.95 = bf16[2,128,128]{2,1,0:T(8,128)(2,1)} custom-call(bf16[2,8,4,4,128,128]{5,4,3,2,1,0:T(8,128)(2,1)} %bitcast.10), custom_call_target="tpu_custom_call" | custom-call | tf_op jit(solution)/shard_map/pallas_call | solution.py:540
  93.2 1.4 %slice_bitcast_fusion = (bf16[128,128]{1,0:T(8,128)(2,1)}, bf16[128,128]{1,0:T(8,128)(2,1)}) fusion(bf16[2,128,128]{2,1,0:T(8,128)(2,1)} %shard_map.95), kind=kLoop, calls=%fused_computation | loop fusion | bytes 131072 | tf_op jit(solution)/shard_map/squeeze | solution.py:776

commit v4 on v3

--- a/solution.py
+++ b/solution.py
@@ -12,6 +12,7 @@
 ROWS = 2 * SPAN
 BLOCK = 512
 UNIT = 512
+STEPS = (4, 2, 1)
 MESH = pl.DeviceIdType.MESH
 AXES = ("z", "y", "x")
 SIZES = {"z": 8, "y": 4, "x": 4}
@@ -20,8 +21,8 @@
 NEAR = (1, -1, 2)
 Z_AWAY = (1, -1, 2, -2, 3, -3, 4)
 GROUPS = ((0,), (1, -1), (2, -2), (3, -3), (4,))
-DIRECT = (4,)
-SUM_DIRECT = (0,)
+DIRECT = (4, 3, -3)
+SUM_DIRECT = (0, 1, -1)
 COPIES = 80
 ZERO_PIECES = 8
 VMEM_BYTES = 60 * 1024 * 1024
@@ -283,7 +284,7 @@
 
 
 def reduce_kernel(
-    terms_ref, out_ref, held, other, final, ring_land, ax_land, ay_land, first_land, second_land,
+    terms_ref, dk_ref, dv_ref, held, other, final, ring_land, ax_land, ay_land, first_land, second_land,
     direct_land, middle_land, z_land, send, recv, load_sem, side_send, side_recv, last_send, last_recv,
 ):
     pos, me, core = my_place()
@@ -522,7 +523,8 @@
     left("ax", ax_land)
     left("ay", ay_land)
     last_copy.wait()
-    out_ref[...] = final[...]
+    dk_ref[...] = final[0]
+    dv_ref[...] = final[1]
 
 
 def reduce_all(terms):
@@ -539,9 +541,9 @@
     one_sem = pltpu.SemaphoreType.DMA
     return pl.pallas_call(
         reduce_kernel,
-        out_shape=jax.ShapeDtypeStruct((2, ROWS, HD), jnp.bfloat16),
+        out_shape=(jax.ShapeDtypeStruct((ROWS, HD), jnp.bfloat16),) * 2,
         in_specs=[pl.BlockSpec(memory_space=pl.ANY)],
-        out_specs=pl.BlockSpec(memory_space=pltpu.VMEM),
+        out_specs=(pl.BlockSpec(memory_space=pltpu.VMEM),) * 2,
         scratch_shapes=[
             vmem(*dims, ROWS),
             vmem(*dims, ROWS),
@@ -568,6 +570,17 @@
     )
 
 
+def over_blocks(count, step, carry):
+    done = jnp.int32(0)
+    for size in STEPS:
+        steps = (count - done) // size
+        carry = lax.fori_loop(
+            0, steps, lambda at, c, done=done, size=size: step(done + at * size, size, c), carry
+        )
+        done = done + steps * size
+    return carry
+
+
 def attention_kernel(
     starts_ref, assign_ref, q_ref, g_ref, kv_ref, zeros_ref, out_ref, dq_ref, terms_ref,
     place_ref, tiles, sums, scores, probs, q_cols, g_cols, acc, in_sem, out_sem,
@@ -652,38 +665,42 @@
         q_cols[...] = q_t.astype(jnp.bfloat16)
         g_cols[...] = g_t.astype(jnp.bfloat16)
 
-        def tile(which, at, part=part):
-            return tiles[part, which, rows_at(at, BLOCK), :]
+        def keys_at(at, size):
+            return pl.ds(pl.multiple_of(at * BLOCK, BLOCK), size * BLOCK)
+
+        def tile(which, at, size, part=part):
+            return tiles[part, which, keys_at(at, size), :]
 
         def fold(value, op):
-            value = value.reshape(BLOCK // 8, 8, cols)
+            value = value.reshape(value.shape[0] // 8, 8, cols)
             return op(value, axis=0)
 
-        def score_step(at, top, part=part):
-            fetched(part, at)
-            s = dot(tile(0, at), q_cols[...], (1, 0))
-            scores[at] = s
+        def score_step(at, size, top, part=part):
+            for i in range(size):
+                fetched(part, at + i)
+            s = dot(tile(0, at, size), q_cols[...], (1, 0))
+            scores[keys_at(at, size), :] = s
             return jnp.maximum(top, fold(s, jnp.max))
 
-        top = lax.fori_loop(0, full_blocks, score_step, jnp.full((8, cols), -1e30, jnp.float32))
+        top = over_blocks(full_blocks, score_step, jnp.full((8, cols), -1e30, jnp.float32))
         fetched(part, full_blocks)
-        s = dot(tile(0, full_blocks), q_cols[...], (1, 0))
+        s = dot(tile(0, full_blocks, 1), q_cols[...], (1, 0))
         key_at = lax.broadcasted_iota(jnp.int32, (BLOCK, cols), 0)
         query_at = lax.broadcasted_iota(jnp.int32, (BLOCK, cols), 1)
         s = jnp.where(key_at <= inside + lax.rem(query_at, SPAN), s, -1e30)
-        scores[full_blocks] = s
+        scores[keys_at(full_blocks, 1), :] = s
         top = jnp.max(jnp.maximum(top, fold(s, jnp.max)), axis=0, keepdims=True)
 
         acc[...] = jnp.zeros_like(acc)
 
-        def value_step(at, total):
-            p = jnp.exp2((scores[at] - top) * to_exp2)
+        def value_step(at, size, total):
+            p = jnp.exp2((scores[keys_at(at, size), :] - top) * to_exp2)
             p16 = p.astype(jnp.bfloat16)
-            probs[at] = p16
-            acc[...] += dot(tile(1, at), p16, (0, 0))
+            probs[keys_at(at, size), :] = p16
+            acc[...] += dot(tile(1, at, size), p16, (0, 0))
             return total + fold(p, jnp.sum)
 
-        total = lax.fori_loop(0, full_blocks + 1, value_step, jnp.zeros((8, cols), jnp.float32))
+        total = over_blocks(full_blocks + 1, value_step, jnp.zeros((8, cols), jnp.float32))
         inverse = 1.0 / jnp.sum(total, axis=0, keepdims=True)
         out_t = (acc[...] * inverse).astype(jnp.bfloat16).astype(jnp.float32)
         delta = jnp.sum(g_t * out_t, axis=0, keepdims=True)
@@ -692,28 +709,30 @@
         out_rows = out_t.T.astype(jnp.bfloat16)
         acc[...] = jnp.zeros_like(acc)
 
-        def grad_step(at, carry, part=part):
-            block = firsts[part] + at
-            p16 = probs[at]
-            keys = tile(0, at)
-            d_probs = dot(tile(1, at), g_cols[...], (1, 0))
+        def grad_step(at, size, carry, part=part):
+            p16 = probs[keys_at(at, size), :]
+            keys = tile(0, at, size)
+            d_probs = dot(tile(1, at, size), g_cols[...], (1, 0))
             d_scores = (as_f32(p16) * (d_probs - delta)).astype(jnp.bfloat16)
             acc[...] += dot(keys, d_scores, (0, 0))
             d_key = dot(d_scores, q_scaled, (1, 1))
             d_value = dot(p16, g_scaled, (1, 1))
-            here = rows_at(block, BLOCK)
-            for which, term in ((0, d_key), (1, d_value)):
+            for i in range(size):
+                block = firsts[part] + at + i
+                here = rows_at(block, BLOCK)
+                for which, term in ((0, d_key), (1, d_value)):
+                    term = term[i * BLOCK : (i + 1) * BLOCK]
+                    if part > 0:
+                        both = (block >= firsts[0]) & (block <= lasts[0])
+                        term = term + jnp.where(both, as_f32(sums[which, here, :]), 0.0)
+                    sums[which, here, :] = term.astype(jnp.bfloat16)
                 if part > 0:
-                    both = (block >= firsts[0]) & (block <= lasts[0])
-                    term = term + jnp.where(both, as_f32(sums[which, here, :]), 0.0)
-                sums[which, here, :] = term.astype(jnp.bfloat16)
-            if part > 0:
-                store(block)
-            else:
-                pl.when(jnp.logical_not(shared(block)))(lambda: store(block))
+                    store(block)
+                else:
+                    pl.when(jnp.logical_not(shared(block)))(lambda block=block: store(block))
             return carry
 
-        lax.fori_loop(0, full_blocks + 1, grad_step, 0)
+        over_blocks(full_blocks + 1, grad_step, 0)
         dq_rows = (acc[...] * (inverse * scale)).T.astype(jnp.bfloat16)
         for h in range(heads):
             out_ref[rows, h * HD : (h + 1) * HD] = out_rows[h * SPAN : (h + 1) * SPAN]
@@ -753,8 +772,8 @@
             pltpu.SMEM(assign.shape, jnp.int32),
             pltpu.VMEM((2, 2, blocks * BLOCK, HD), jnp.bfloat16),
             pltpu.VMEM((2, tokens, HD), jnp.bfloat16),
-            pltpu.VMEM((blocks, BLOCK, cols), jnp.float32),
-            pltpu.VMEM((blocks, BLOCK, cols), jnp.bfloat16),
+            pltpu.VMEM((blocks * BLOCK, cols), jnp.float32),
+            pltpu.VMEM((blocks * BLOCK, cols), jnp.bfloat16),
             pltpu.VMEM((HD, cols), jnp.bfloat16),
             pltpu.VMEM((HD, cols), jnp.bfloat16),
             pltpu.VMEM((HD, cols), jnp.float32),
@@ -772,8 +791,8 @@
     attn_out, d_query, terms = attention(
         doc_starts, assign, queries, d_out, kv_all.reshape(2, tokens, HD), zeros.reshape(2, tokens, HD)
     )
-    summed = reduce_all(terms.reshape(2, *dims, ROWS, HD))
-    return (attn_out, d_query, summed[0], summed[1])
+    d_key, d_value = reduce_all(terms.reshape(2, *dims, ROWS, HD))
+    return (attn_out, d_query, d_key, d_value)
 
 
 def solution(mesh):

time: 94.8 us -> 93.8 us (0.989)
  Pallas kernels: 92.5 us -> 90.1 us
  local copies, waits for them, and re-layouts: 1.4 us -> 2.75 us
    unnamed x0 -> x2, local copies, waits for them, and re-layouts: none -> 2.75 us
    squeeze x1 -> x0, local copies, waits for them, and re-layouts: 1.4 us -> none  [body(): return (attn_out, d_query, summed[0], summed[1])]
    pallas_call x1, Pallas kernels: 40.7 us -> 39.3 us  [gather_all(): pl.pallas_call(gather_kernel, out_shape=(jax.ShapeDtypeStruct((2, *dims,...]
    pallas_call x1, Pallas kernels: 44.1 us -> 42.8 us  [reduce_all(): pl.pallas_call(reduce_kernel, out_shape=(jax.ShapeDtypeStruct((ROWS, HD),...]
where the time goes in v4:
time: 93.8 us; the launch traced here: 93.5 us
  Pallas kernels  90.1 us (96%)
  local copies, waits for them, and re-layouts  2.75 us (3%)
    pallas_call x1, Pallas kernels, reduce_all(): pl.pallas_call(reduce_kernel, out_shape=(jax.ShapeDtypeStruct((ROWS, HD),...  42.8 us
    pallas_call x1, Pallas kernels, gather_all(): pl.pallas_call(gather_kernel, out_shape=(jax.ShapeDtypeStruct((2, *dims,...  39.3 us
    pallas_call x1, Pallas kernels, attention(): pl.pallas_call(attention_kernel, out_shape=(jax.ShapeDtypeStruct(queries....  7.98 us
    unnamed x2, local copies, waits for them, and re-layouts  2.75 us

profile of v4, /device:TPU:1, one launch (start us, length us, event | category | flops | bytes accessed | tf_op | source)
XLA Modules:
  0.0 93.5 jit_solution(18343623967356498206)
XLA Ops:
  0.6 39.3 %shard_map.93 = (bf16[2,8,4,4,128,128]{5,4,3,2,1,0:T(8,128)(2,1)}, bf16[32768,128]{1,0:T(8,128)(2,1)}) custom-call(bf16[1,1,1,128,128]{4,3,2,1,0:T(8,128)(2,1)} %bitcast.8, bf16[1,1,1,128,128]{4,3,2,1,0:T(8,128)(2,1)} %bitcast.9), custom_call_target="tpu_custom_call" | custom-call | tf_op jit(solution)/shard_map/pallas_call | solution.py:270
  40.0 8.0 %shard_map.94 = (bf16[128,1024]{1,0:T(8,128)(2,1)}, bf16[128,1024]{1,0:T(8,128)(2,1)}, bf16[2,16384,128]{2,1,0:T(8,128)(2,1)}) custom-call(s32[16]{0:T(128)} %starts_ref.1, s32[256]{0:T(256)} %assign_ref.1, bf16[128,1024]{1,0:T(8,128)(2,1)} %q_ref.1, bf16[128,1024]{1,0:T(8,128)(2,1)} %g_ref.1, ...), custom_call_target="tpu_custom_call", output_to_operand_aliasing={{2}: (5, {})} | custom-call | tf_op jit(solution)/shard_map/pallas_call | solution.py:761
  48.0 42.8 %shard_map.95 = (bf16[128,128]{1,0:T(8,128)(2,1)}, bf16[128,128]{1,0:T(8,128)(2,1)}) custom-call(bf16[2,8,4,4,128,128]{5,4,3,2,1,0:T(8,128)(2,1)} %bitcast.6), custom_call_target="tpu_custom_call" | custom-call | tf_op jit(solution)/shard_map/pallas_call | solution.py:542
  90.8 1.4 %copy.14 = bf16[128,128]{1,0:T(8,128)(2,1)} copy(bf16[128,128]{1,0:T(8,128)(2,1)} %get-tuple-element.24) | data formatting | bytes 65536
  92.1 1.4 %copy.15 = bf16[128,128]{1,0:T(8,128)(2,1)} copy(bf16[128,128]{1,0:T(8,128)(2,1)} %get-tuple-element.25) | data formatting | bytes 65536

commit v5 on v4

--- a/solution.py
+++ b/solution.py
@@ -23,7 +23,7 @@
 GROUPS = ((0,), (1, -1), (2, -2), (3, -3), (4,))
 DIRECT = (4, 3, -3)
 SUM_DIRECT = (0, 1, -1)
-COPIES = 80
+COPIES = 74
 ZERO_PIECES = 8
 VMEM_BYTES = 60 * 1024 * 1024
 
@@ -284,7 +284,7 @@
 
 
 def reduce_kernel(
-    terms_ref, dk_ref, dv_ref, held, other, final, ring_land, ax_land, ay_land, first_land, second_land,
+    terms_ref, out_ref, held, other, final, ring_land, ax_land, ay_land, first_land, second_land,
     direct_land, middle_land, z_land, send, recv, load_sem, side_send, side_recv, last_send, last_recv,
 ):
     pos, me, core = my_place()
@@ -478,10 +478,6 @@
             for route in both:
                 for d in far_first[at]:
                     send_first(route, d)
-            ring(at + 1)
-        if at == len(far_first) - 1:
-            for m in NEAR:
-                push(*ax_copy(m))
         for behind, act in ((1, send_second), (2, send_middle), (3, send_z)):
             for begun, group in enumerate(far_first):
                 for d in group:
@@ -489,6 +485,11 @@
                     if begun + behind - sooner == at and not (sooner and act is send_second):
                         for route in both:
                             act(route, d)
+        if at < len(far_first):
+            ring(at + 1)
+        if at == len(far_first) - 1:
+            for m in NEAR:
+                push(*ax_copy(m))
         if at == len(far_first):
             arrived(("ax",), ax_land)
             for y in range(SIZES["y"]):
@@ -523,8 +524,7 @@
     left("ax", ax_land)
     left("ay", ay_land)
     last_copy.wait()
-    dk_ref[...] = final[0]
-    dv_ref[...] = final[1]
+    out_ref[...] = final[...]
 
 
 def reduce_all(terms):
@@ -541,9 +541,9 @@
     one_sem = pltpu.SemaphoreType.DMA
     return pl.pallas_call(
         reduce_kernel,
-        out_shape=(jax.ShapeDtypeStruct((ROWS, HD), jnp.bfloat16),) * 2,
+        out_shape=jax.ShapeDtypeStruct((2, ROWS, HD), jnp.bfloat16),
         in_specs=[pl.BlockSpec(memory_space=pl.ANY)],
-        out_specs=(pl.BlockSpec(memory_space=pltpu.VMEM),) * 2,
+        out_specs=pl.BlockSpec(memory_space=pltpu.VMEM),
         scratch_shapes=[
             vmem(*dims, ROWS),
             vmem(*dims, ROWS),
@@ -791,8 +791,8 @@
     attn_out, d_query, terms = attention(
         doc_starts, assign, queries, d_out, kv_all.reshape(2, tokens, HD), zeros.reshape(2, tokens, HD)
     )
-    d_key, d_value = reduce_all(terms.reshape(2, *dims, ROWS, HD))
-    return (attn_out, d_query, d_key, d_value)
+    summed = reduce_all(terms.reshape(2, *dims, ROWS, HD))
+    return (attn_out, d_query, summed[0], summed[1])
 
 
 def solution(mesh):

time: 93.8 us -> 93.9 us (level)
  local copies, waits for them, and re-layouts: 2.75 us -> 1.4 us
    unnamed x2 -> x0, local copies, waits for them, and re-layouts: 2.75 us -> none
    pallas_call x1, Pallas kernels: 7.98 us -> 10.7 us  [attention(): pl.pallas_call(attention_kernel, out_shape=(jax.ShapeDtypeStruct(queries....]
    pallas_call x1, Pallas kernels: 42.8 us -> 41 us  [reduce_all(): pl.pallas_call(reduce_kernel, out_shape=jax.ShapeDtypeStruct((2, ROWS, HD...]
    squeeze x0 -> x1, local copies, waits for them, and re-layouts: none -> 1.4 us  [body(): return (attn_out, d_query, summed[0], summed[1])]
where the time goes in v5:
time: 93.9 us; the launch traced here: 93 us
  Pallas kernels  91 us (97%)
  local copies, waits for them, and re-layouts  1.4 us (1%)
    pallas_call x1, Pallas kernels, reduce_all(): pl.pallas_call(reduce_kernel, out_shape=jax.ShapeDtypeStruct((2, ROWS, HD...  41 us
    pallas_call x1, Pallas kernels, gather_all(): pl.pallas_call(gather_kernel, out_shape=(jax.ShapeDtypeStruct((2, *dims,...  39.3 us
    pallas_call x1, Pallas kernels, attention(): pl.pallas_call(attention_kernel, out_shape=(jax.ShapeDtypeStruct(queries....  10.7 us

profile of v5, /device:TPU:1, one launch (start us, length us, event | category | flops | bytes accessed | tf_op | source)
XLA Modules:
  0.0 93.0 jit_solution(12098021836888307032)
XLA Ops:
  0.6 39.3 %shard_map.93 = (bf16[2,8,4,4,128,128]{5,4,3,2,1,0:T(8,128)(2,1)}, bf16[32768,128]{1,0:T(8,128)(2,1)}) custom-call(bf16[1,1,1,128,128]{4,3,2,1,0:T(8,128)(2,1)} %bitcast.12, bf16[1,1,1,128,128]{4,3,2,1,0:T(8,128)(2,1)} %bitcast.13), custom_call_target="tpu_custom_call" | custom-call | tf_op jit(solution)/shard_map/pallas_call | solution.py:270
  39.9 10.7 %shard_map.94 = (bf16[128,1024]{1,0:T(8,128)(2,1)}, bf16[128,1024]{1,0:T(8,128)(2,1)}, bf16[2,16384,128]{2,1,0:T(8,128)(2,1)}) custom-call(s32[16]{0:T(128)} %starts_ref.1, s32[256]{0:T(256)} %assign_ref.1, bf16[128,1024]{1,0:T(8,128)(2,1)} %q_ref.1, bf16[128,1024]{1,0:T(8,128)(2,1)} %g_ref.1, ...), custom_call_target="tpu_custom_call", output_to_operand_aliasing={{2}: (5, {})} | custom-call | tf_op jit(solution)/shard_map/pallas_call | solution.py:761
  50.6 41.0 %shard_map.95 = bf16[2,128,128]{2,1,0:T(8,128)(2,1)} custom-call(bf16[2,8,4,4,128,128]{5,4,3,2,1,0:T(8,128)(2,1)} %bitcast.10), custom_call_target="tpu_custom_call" | custom-call | tf_op jit(solution)/shard_map/pallas_call | solution.py:542
  91.6 1.4 %slice_bitcast_fusion = (bf16[128,128]{1,0:T(8,128)(2,1)}, bf16[128,128]{1,0:T(8,128)(2,1)}) fusion(bf16[2,128,128]{2,1,0:T(8,128)(2,1)} %shard_map.95), kind=kLoop, calls=%fused_computation | loop fusion | bytes 131072 | tf_op jit(solution)/shard_map/squeeze | solution.py:795
